TPU v7x, 32 devices: a whole 2x2x4 slice. The times are simulated.
32 devices in a mesh: dp: 16 (over z, x, core), cent: 2 (over y).
Axes of the slice: x: 2, y: 2, z: 4, core: 2. Of those that a mesh axis runs over, the one named last changes fastest.
Arguments:
- vectors: bfloat16 [16384, 768], P('dp'), may hold values from -64 to 64
- centroids: bfloat16 [8192, 768], P('cent'), may hold values from -5 to 5
- prior_mass: float32 [8192], P('cent'), may hold values from 0.5 to 8
- assign: int32 [16384], P('dp'), may hold values from 0 to 8191, as said below
- owner_of: int32 [8192], replicated, may hold values from 0 to 15, as said below
- rotation: bfloat16 [768, 768], replicated, may hold values from -0.21875 to 0.21875
Outputs:
- new_centroids: float32 [2, 4096, 768], P('cent', 'dp')
- moments: float32 [16, 16, 768], P('dp', None, 'cent')
Inputs may be any that keep to these rules, and one draw needn't show every extreme that they name: `assign`: of the 1024 vectors of each dp index, exactly 512 have their list in each block of 4096 consecutive lists; of those, at most 128 have lists of one owner, and for each block of lists one owner, the same for every dp index, receives exactly 128 from every dp index. `owner_of`: each owner holds exactly 256 lists of each block of 4096 consecutive lists.
All inputs are finite; a program needn't handle non-finite values.
Results may differ from a plain program's by a relative error of at most 0.0033.
Values may be sent and summed in bfloat16 or wider, within the bound.
No kernel may reach another device: no remote copies, remote signals or barrier semaphores. Data moves between devices by JAX's collectives and lax.ppermute only.
A program may use at most 64 MiB of HBM per device.

v0:
```python
import math

import jax
import jax.numpy as jnp
from jax import lax
from jax.sharding import PartitionSpec as P

M = 48


def combined_all(array, axis, combine):
    everything = jax.tree.map(lambda part: lax.all_gather(part, axis), array)
    leading = jax.tree.map(lambda part: part[0], everything)

    def turn(k, so_far):
        return combine(so_far, jax.tree.map(lambda part: part[k], everything))

    return lax.fori_loop(1, lax.axis_size(axis), turn, leading)


def peak_merge(earlier, later):
    top_val = jnp.maximum(earlier[0], later[0])
    merged = earlier[1] * jnp.exp(earlier[0] - top_val) + later[1] * jnp.exp(later[0] - top_val)
    return (top_val, merged)


def body(vectors, centroids, prior_mass, assign, owner_of, rotation):
    feat_width = vectors.shape[1]
    shard_rows = centroids.shape[0]
    cent_count = lax.axis_size("cent")
    owner_count = lax.axis_size("dp")
    cent_pos = lax.axis_index("cent")
    dp_pos = lax.axis_index("dp")
    inv_root = 1.0 / math.sqrt(feat_width)
    cent_square = jnp.sum(jnp.square(centroids.astype(jnp.float32)), axis=1)
    cross_dot = lax.dot_general(
        vectors, centroids, (((1,), (1,)), ((), ())), preferred_element_type=jnp.float32
    )
    scores = (2.0 * cross_dot - cent_square[None, :]) * inv_root
    local_peak = jnp.max(scores, axis=1)
    local_exp = jnp.exp(scores - local_peak[:, None])
    peak_val, row_total = combined_all((local_peak, jnp.sum(local_exp, axis=1)), "cent", peak_merge)
    factor = jnp.exp(local_peak - peak_val) / row_total
    member_prob = (local_exp * factor[:, None]).astype(jnp.bfloat16)
    sum_rows = lax.dot_general(
        member_prob, vectors, (((0,), (0,)), ((), ())), preferred_element_type=jnp.float32
    )
    soft_mass = jnp.sum(member_prob, axis=0, dtype=jnp.float32)
    own_count = shard_rows // owner_count
    own_sums, own_mass = (
        lax.psum_scatter(sum_rows, "dp", scatter_dimension=0, tiled=True),
        lax.psum_scatter(soft_mass, "dp", scatter_dimension=0, tiled=True),
    )
    own_cent = lax.dynamic_slice_in_dim(centroids, dp_pos * own_count, own_count, 0).astype(
        jnp.float32
    )
    own_prior = lax.dynamic_slice_in_dim(prior_mass, dp_pos * own_count, own_count, 0)
    updated = (own_prior[:, None] * own_cent + own_sums) / (own_prior + own_mass)[:, None]
    row_count = assign.shape[0]
    per_shard = row_count // cent_count
    slot_cap = 4 * per_shard // owner_count
    inside = assign // shard_rows == cent_pos
    in_rank = jnp.cumsum(inside.astype(jnp.int32)) - 1
    target = jnp.where(inside, in_rank, per_shard)
    picked = (
        jnp.zeros((per_shard,), jnp.int32)
        .at[target]
        .set(jnp.arange(row_count, dtype=jnp.int32), mode="drop")
    )
    list_ids = assign[picked]
    owners = owner_of[list_ids]
    local_list = list_ids - cent_pos * shard_rows
    residual = (
        vectors[picked].astype(jnp.float32) - centroids[local_list].astype(jnp.float32)
    ).astype(jnp.bfloat16)
    member = (owners[:, None] == jnp.arange(owner_count, dtype=jnp.int32)[None, :]).astype(
        jnp.int32
    )
    in_order = jnp.sum(jnp.cumsum(member, axis=0) * member, axis=1) - 1
    slot_ids = owners * slot_cap + in_order
    empty_rows = jnp.zeros((owner_count * slot_cap, feat_width), jnp.bfloat16)
    packed = empty_rows.at[slot_ids].set(residual).reshape(owner_count, slot_cap, feat_width)
    turned = jnp.einsum(
        "smd,de->sme",
        lax.all_to_all(packed, "dp", split_axis=0, concat_axis=0, tiled=True),
        rotation,
        preferred_element_type=jnp.float32,
    )
    rotated = turned.astype(jnp.bfloat16)
    sub_width = feat_width // M
    flat_rows = rotated.reshape(owner_count * slot_cap, M, sub_width)
    per_space = jnp.transpose(flat_rows, (1, 0, 2))
    local_moments = lax.dot_general(
        per_space, per_space, (((1,), (1,)), ((0,), (0,))), preferred_element_type=jnp.float32
    )
    local_moments = jnp.transpose(local_moments, (1, 0, 2)).reshape(sub_width, feat_width)
    moment_part = lax.psum_scatter(local_moments, "cent", scatter_dimension=1, tiled=True)
    moment_part = moment_part / vectors.shape[0]
    return (updated[None], moment_part[None])


def solution(mesh):
    return jax.shard_map(
        body,
        mesh=mesh,
        in_specs=(P("dp", None), P("cent", None), P("cent"), P("dp"), P(), P()),
        out_specs=(P("cent", "dp", None), P("dp", None, "cent")),
        check_vma=False,
    )
```

profile of v0, /device:TPU:0, one launch (start us, length us, event | category | flops | bytes accessed | tf_op | source)
XLA Modules:
  0.0 291.0 jit_solution(85697500171727103)
XLA Ops:
  7.2 0.0 copy-start
  7.2 0.8 convert_bitcast_fusion
  8.0 0.3 reduce-window.15
  8.3 0.1 slice.23
  8.4 0.1 slice_reduce_fusion.1
  8.5 0.1 compare_select_fusion.3
  8.6 4.3 %scatter_custom_fusion = s32[512]{0:T(512)S(1)} fusion(s32[1024]{0:T(1024)S(1)} %compare_select_fusion.3, s32[1024]{0:T(1024)S(1)} %iota.11, s32[]{:T(128)} %constant.26.clone.1), kind=kCustom, calls=%fused_computation.58 | custom fusion | bytes 2052 | tf_op jit(solution)/shard_map/scatter | solution.py:68
  12.9 3.4 %gather_fusion = s32[512]{0:T(512)S(1)} fusion(s32[1024]{0:T(1024)} %param.9, s32[1024]{0:T(1024)S(1)} %pad_clamp_fusion.2), kind=kCustom, calls=%fused_computation | custom fusion | bytes 6144 | tf_op jit(solution)/shard_map/gather | solution.py:70
  16.3 3.4 %gather_fusion.1 = s32[512]{0:T(512)S(1)} fusion(s32[8192]{0:T(1024)} %param.10, s32[1024]{0:T(1024)S(1)} %pad_clamp_fusion.1), kind=kCustom, calls=%fused_computation.1 | custom fusion | bytes 6144 | tf_op jit(solution)/shard_map/gather | solution.py:71
  19.8 1.2 reduce-window.19
  20.9 0.2 slice_reduce_fusion
  21.2 0.1 fusion.11
  21.3 0.0 copy-done
  21.3 11.7 %scatter_custom_fusion.1 = bf16[2048,768]{1,0:T(8,128)(2,1)} fusion(s32[512]{0:T(512)S(1)} %bitcast.56, bf16[]{:T(256)} %constant.64.clone.1, bf16[4096,768]{1,0:T(8,128)(2,1)} %param.7, s32[1024]{0:T(1024)S(1)} %pad_clamp_fusion, bf16[1024,768]{1,0:T(8,128)(2,1)S(1)} %copy-done, s32[1024]{0:T(1024)S(1)} %pad_clamp_fusion.2), kind=kCustom, calls=%fused_computation.17 | custom fusion | flops 1572864 | bytes 11018242 | tf_op jit(solution)/shard_map/scatter | solution.py:82
  33.1 7.4 %all-to-all-start = ((bf16[16,128,768]{2,1,0:T(8,128)(2,1)}), bf16[16,128,768]{2,1,0:T(8,128)(2,1)}, u32[]{:S(2)}, u32[]{:S(2)}) async-start(bf16[16,128,768]{2,1,0:T(8,128)(2,1)} %bitcast.50), calls=%async_computation.1 | async-start | bytes 6291456 | tf_op jit(solution)/shard_map/all_to_all | solution.py:85
  40.5 0.0 reduce-scatter.5.cloned.1.call-start
  40.5 4.1 %multiply_reduce_fusion = f32[4096]{0:T(1024)S(1)} fusion(bf16[4096,768]{1,0:T(8,128)(2,1)} %param.7), kind=kLoop, calls=%fused_computation.11 | loop fusion | flops 9433088 | bytes 6307840 | tf_op jit(solution)/shard_map/reduce_sum | solution.py:35
  44.6 9.1 %fusion.1 = (f32[1024]{0:T(1024)S(1)}, f32[1024,4096]{1,0:T(8,128)S(1)}) fusion(f32[4096]{0:T(1024)S(1)} %multiply_reduce_fusion, bf16[1024,768]{1,0:T(8,128)(2,1)S(1)} %copy-done, bf16[4096,768]{1,0:T(8,128)(2,1)} %param.7), kind=kOutput, calls=%fused_computation.12 | convolution fusion | flops 6459227136 | bytes 24662016 | tf_op jit(solution)/shard_map/dot_general | solution.py:36
  53.7 4.3 %all-gather = f32[2048]{0:T(1024)S(1)} all-gather(f32[1024]{0:T(1024)S(1)} %get-tuple-element.28), channel_id=2, replica_groups=mesh['dp'=16,'cent'=2] {'cent'}, dimensions={0}, use_global_device_ids=true | all-gather | bytes 12288 | tf_op jit(solution)/shard_map/all_gather | solution.py:12
  58.0 4.5 %fusion = f32[1024]{0:T(1024)S(1)} fusion(f32[1024,4096]{1,0:T(8,128)S(1)} %get-tuple-element.29, f32[1024]{0:T(1024)S(1)} %get-tuple-element.28, f32[4096]{0:T(1024)S(1)} %multiply_reduce_fusion), kind=kLoop, calls=%fused_computation.10 | loop fusion | flops 20970496 | bytes 16801792 | tf_op jit(solution)/shard_map/reduce_sum | solution.py:42
  62.6 4.3 %all-gather.1 = f32[2048]{0:T(1024)S(1)} all-gather(f32[1024]{0:T(1024)S(1)} %fusion), channel_id=3, replica_groups=mesh['dp'=16,'cent'=2] {'cent'}, dimensions={0}, use_global_device_ids=true | all-gather | bytes 12288 | tf_op jit(solution)/shard_map/all_gather | solution.py:12
  66.9 0.0 copy-start.1
  66.9 7.1 %convert_reduce_fusion = (f32[4096]{0:T(1024)S(1)}, bf16[1024,4096]{1,0:T(8,128)(2,1)}) fusion(f32[1024]{0:T(1024)S(1)} %fusion.16, f32[1024]{0:T(1024)S(1)} %get-tuple-element.28, f32[4096]{0:T(1024)S(1)} %multiply_reduce_fusion, f32[1024,4096]{1,0:T(8,128)S(1)} %get-tuple-element.29), kind=kLoop, calls=%fused_computation.6 | loop fusion | flops 33550336 | bytes 25206784 | tf_op jit(solution)/shard_map/reduce_sum | solution.py:48
  74.1 25.8 %all-to-all-done = bf16[16,128,768]{2,1,0:T(8,128)(2,1)} async-done(((bf16[16,128,768]{2,1,0:T(8,128)(2,1)}), bf16[16,128,768]{2,1,0:T(8,128)(2,1)}, u32[]{:S(2)}, u32[]{:S(2)}) %all-to-all-start) | async-done | bytes 3145760 | tf_op jit(solution)/shard_map/all_to_all | solution.py:85
  99.9 0.0 copy-done.1
  99.9 6.2 %convolution_convert_fusion = bf16[16,128,768]{2,1,0:T(8,128)(2,1)} fusion(bf16[16,128,768]{2,1,0:T(8,128)(2,1)} %all-to-all-done, bf16[768,768]{1,0:T(8,128)(2,1)S(1)} %copy-done.1), kind=kOutput, calls=%fused_computation.15 | convolution fusion | flops 2417491968 | bytes 7471104 | tf_op jit(solution)/shard_map/smd,de->sme/dot_general | solution.py:83
  106.1 5.1 %copy.13 = bf16[16,128,768]{1,0,2:T(8,128)(2,1)} copy(bf16[16,128,768]{2,1,0:T(8,128)(2,1)} %convolution_convert_fusion) | data formatting | bytes 6291456 | tf_op jit(solution)/shard_map/convert_element_type | solution.py:89
  111.2 5.8 %reshape.149 = bf16[2048,48,16]{0,2,1:T(8,128)(2,1)} reshape(bf16[16,128,768]{1,0,2:T(8,128)(2,1)} %copy.13) | data formatting | bytes 6291456 | tf_op jit(solution)/shard_map/reshape | solution.py:91
  117.0 4.3 %fusion.6 = f32[16,48,16]{2,0,1:T(8,128)S(1)} fusion(bf16[2048,48,16]{0,2,1:T(8,128)(2,1)} %reshape.149), kind=kOutput, calls=%fused_computation.19 | convolution fusion | flops 50331648 | bytes 3194880 | tf_op jit(solution)/shard_map/dot_general | solution.py:93
  121.3 0.1 copy.14
  121.4 0.8 reshape.150
  122.2 0.0 reduce-scatter.5.cloned.1.call-update
  122.3 0.3 reduce-scatter.3.cloned.1.call-start
  122.5 12.9 %fusion.24 = f32[4096,768]{1,0:T(8,128)} fusion(bf16[1024,4096]{1,0:T(8,128)(2,1)} %get-tuple-element.25, bf16[1024,768]{1,0:T(8,128)(2,1)S(1)} %copy-done), kind=kOutput, calls=%fused_computation.62 | convolution fusion | flops 6442450944 | bytes 22544384 | tf_op jit(solution)/shard_map/dot_general | solution.py:45
  135.4 0.0 copy-start.2
  135.4 0.0 reduce-scatter.3.cloned.1.call-update
  135.4 0.6 copy-done.2
  136.0 0.6 dynamic-slice
  137.3 73.1 %all-reduce = f32[4096]{0:T(1024)S(1)} all-reduce(f32[4096]{0:T(1024)S(1)} %get-tuple-element.24), channel_id=5, replica_groups=mesh['dp'=16,'cent'=2] {'dp'}, use_global_device_ids=true, to_apply=%region_5.0.clone | all-reduce | flops 4096 | bytes 32768
  210.4 0.8 dynamic-slice_add_fusion
  211.2 0.0 reduce-scatter.5.cloned.1.call-done
  211.2 1.4 multiply_bitcast_fusion
  212.5 69.4 %reduce-scatter.3.cloned.1.call-done = f32[256,768]{1,0:T(8,128)} async-done(((f32[4096,768]{1,0:T(8,128)}), f32[256,768]{1,0:T(8,128)}) %reduce-scatter.3.cloned.1.call-update) | async-done | bytes 786448 | tf_op jit(solution)/shard_map/reduce_scatter | solution.py:51
  281.9 2.3 divide_bitcast_fusion
  (13 shorter events, 0.1 us)
Async XLA Ops:
  7.2 14.2 %copy-start = (bf16[1024,768]{1,0:T(8,128)(2,1)S(1)}, bf16[1024,768]{1,0:T(8,128)(2,1)}, u32[]{:S(2)}) copy-start(bf16[1024,768]{1,0:T(8,128)(2,1)} %param.6) | copy-start | bytes 4718596
  33.1 66.8 %all-to-all-start = ((bf16[16,128,768]{2,1,0:T(8,128)(2,1)}), bf16[16,128,768]{2,1,0:T(8,128)(2,1)}, u32[]{:S(2)}, u32[]{:S(2)}) async-start(bf16[16,128,768]{2,1,0:T(8,128)(2,1)} %bitcast.50), calls=%async_computation.1 | async-start | bytes 6291456 | tf_op jit(solution)/shard_map/all_to_all | solution.py:85
  40.5 170.7 %reduce-scatter.5.cloned.1.call-start = ((), (), s32[]{:S(2)}) async-start(), calls=%async_computation.4 | async-start | bytes 73728 | tf_op jit(solution)/shard_map/reduce_scatter | solution.py:97
  66.9 33.0 %copy-start.1 = (bf16[768,768]{1,0:T(8,128)(2,1)S(1)}, bf16[768,768]{1,0:T(8,128)(2,1)}, u32[]{:S(2)}) copy-start(bf16[768,768]{1,0:T(8,128)(2,1)} %param.11) | copy-start | bytes 3538948
  122.3 159.6 %reduce-scatter.3.cloned.1.call-start = ((), (), s32[]{:S(2)}) async-start(), calls=%async_computation.3 | async-start | bytes 13369344 | tf_op jit(solution)/shard_map/reduce_scatter | solution.py:51
  135.4 0.7 copy-start.2
Sparse Core Ops, SparseCore 0:
  122.4 20.6 reduce-scatter.4
  147.1 134.7 reduce-scatter.2
where the time goes:
time: 292 us; the launch traced here: 291 us
  waiting for transfers between devices  95.2 us (33%)
  blocking collectives  81.8 us (28%)
  other arithmetic  34.4 us (12%)
  matrix products  32.4 us (11%)
  local copies, waits for them, and re-layouts  24.6 us (8%)
  between operations  14.8 us (5%)
  starting transfers between devices  7.72 us (3%)
    unnamed x1, blocking collectives  73.1 us
    reduce_scatter x1, waiting for transfers between devices, body(): lax.psum_scatter(sum_rows, 'dp', scatter_dimension=0, tiled=True)  69.4 us
    all_to_all x1, waiting for transfers between devices, body(): lax.all_to_all(packed, 'dp', split_axis=0, concat_axis=0, tiled=True)  25.8 us
    dot_general x1, matrix products, body(): lax.dot_general(member_prob, vectors, (((0,), (0,)), ((), ())), preferred...  12.9 us
    scatter x1, other arithmetic, body(): empty_rows.at[slot_ids].set(residual)  11.7 us
    dot_general x1, matrix products, body(): lax.dot_general(vectors, centroids, (((1,), (1,)), ((), ())), preferred_e...  9.07 us
    all_gather x2, blocking collectives, combined_all(): everything = jax.tree.map(lambda part: lax.all_gather(part, axis), array)  8.68 us
    all_to_all x1, starting transfers between devices, body(): lax.all_to_all(packed, 'dp', split_axis=0, concat_axis=0, tiled=True)  7.41 us
  transfers between devices with their start and end apart: 3, of which 2 were waited for; matrix products, arithmetic and copies ran while one was open for 14% of the time, Pallas kernels for 0%

commit v1 on v0

v1 whole, which is shorter than its diff:
```python
import functools
import math

import jax
import jax.numpy as jnp
from jax import lax
from jax.experimental import pallas as pl
from jax.experimental.pallas import tpu as pltpu
from jax.sharding import PartitionSpec as P

M = 48
VMEM_LIMIT = 56 * 1024 * 1024
F32 = jnp.float32
BF16 = jnp.bfloat16


def params(steps=1):
    return pltpu.CompilerParams(
        dimension_semantics=("arbitrary",) * steps, vmem_limit_bytes=VMEM_LIMIT
    )


def dot(a, b, ca, cb):
    return lax.dot_general(a, b, (((ca,), (cb,)), ((), ())), preferred_element_type=F32)


def score_kernel(ids_ref, v_ref, c_ref, s_ref, st_ref, vt_ref, *, scale):
    step = pl.program_id(0)

    @pl.when(step == 0)
    def _():
        vt_ref[...] = v_ref[...].T
        st_ref[...] = jnp.zeros_like(st_ref)
        st_ref[0:1, :] = jnp.full((1, st_ref.shape[1]), -jnp.inf, F32)

    c = c_ref[0]
    c32 = c.astype(F32)
    square = jnp.sum(c32 * c32, axis=1, keepdims=True) * scale
    s = dot(c, vt_ref[...], 1, 0) * (2.0 * scale) - square
    s_ref[0] = s
    old_peak = st_ref[0:1, :]
    peak = jnp.maximum(old_peak, jnp.max(s, axis=0, keepdims=True))
    part = jnp.sum(jnp.exp2(s - peak), axis=0, keepdims=True)
    st_ref[1:2, :] = st_ref[1:2, :] * jnp.exp2(old_peak - peak) + part
    st_ref[0:1, :] = peak


def scores_of(ids, v, c_blocks, scale):
    n, (_, rows, width) = ids.shape[0], c_blocks.shape
    count = v.shape[0]
    return pl.pallas_call(
        functools.partial(score_kernel, scale=scale),
        grid_spec=pltpu.PrefetchScalarGridSpec(
            num_scalar_prefetch=1,
            grid=(n,),
            in_specs=[
                pl.BlockSpec((count, width), lambda i, ids: (0, 0)),
                pl.BlockSpec((1, rows, width), lambda i, ids: (ids[i], 0, 0)),
            ],
            out_specs=[
                pl.BlockSpec((1, rows, count), lambda i, ids: (i, 0, 0)),
                pl.BlockSpec((8, count), lambda i, ids: (0, 0)),
            ],
            scratch_shapes=[pltpu.VMEM((width, count), BF16)],
        ),
        out_shape=[
            jax.ShapeDtypeStruct((n, rows, count), F32),
            jax.ShapeDtypeStruct((8, count), F32),
        ],
        compiler_params=params(),
        cost_estimate=pl.CostEstimate(
            flops=2 * n * rows * width * count,
            bytes_accessed=4 * n * rows * count,
            transcendentals=n * rows * count,
        ),
        name="scores",
    )(ids, v, c_blocks)


def sums_kernel(s1_ref, s2_ref, st_ref, v1_ref, v2_ref, o_ref, m_ref):
    def resp(s_ref, row):
        peak, inverse = st_ref[row : row + 1, :], st_ref[row + 1 : row + 2, :]
        return (jnp.exp2(s_ref[0] - peak) * inverse).astype(BF16)

    r1, r2 = resp(s1_ref, 0), resp(s2_ref, 2)
    o_ref[0] = (dot(r1, v1_ref[...], 1, 0) + dot(r2, v2_ref[...], 1, 0)).astype(o_ref.dtype)
    both = r1.astype(F32) + r2.astype(F32)
    rows, count = both.shape
    lanes = 128 if count % 128 == 0 else count
    part = both[:, :lanes]
    for k in range(lanes, count, lanes):
        part = part + both[:, k : k + lanes]
    m_ref[0] = jnp.sum(part.T, axis=0, keepdims=True)


def sums_of(s1, s2, stats, v1, v2, first, n, out_dtype):
    _, rows, count = s1.shape
    width = v1.shape[1]
    score_spec = pl.BlockSpec((1, rows, count), lambda i: (first + i, 0, 0))
    v_spec = pl.BlockSpec((count, width), lambda i: (0, 0))
    return pl.pallas_call(
        sums_kernel,
        grid=(n,),
        in_specs=[score_spec, score_spec, pl.BlockSpec((4, count), lambda i: (0, 0)), v_spec, v_spec],
        out_specs=[
            pl.BlockSpec((1, rows, width), lambda i: (i, 0, 0)),
            pl.BlockSpec((1, 1, rows), lambda i: (i, 0, 0)),
        ],
        out_shape=[
            jax.ShapeDtypeStruct((n, rows, width), out_dtype),
            jax.ShapeDtypeStruct((n, 1, rows), F32),
        ],
        compiler_params=params(),
        cost_estimate=pl.CostEstimate(
            flops=4 * n * rows * width * count,
            bytes_accessed=8 * n * rows * count,
            transcendentals=2 * n * rows * count,
        ),
        name="sums",
    )(s1, s2, stats, v1, v2)


def residual_kernel(
    list_ref, v_ref, c_ref, owner_ref, rot_ref, r_ref, own_ref, picked_ref, ids_ref, acc_ref
):
    step = pl.program_id(0)
    per_shard, width = picked_ref.shape
    row_count = v_ref.shape[0]
    chunk = c_ref.shape[0]

    @pl.when(step == 0)
    def _():
        lists = list_ref[...]
        inside = lists >= 0
        upper = lax.broadcasted_iota(jnp.int32, (row_count, row_count), 0) <= (
            lax.broadcasted_iota(jnp.int32, (row_count, row_count), 1)
        )
        flags = jnp.broadcast_to(inside.astype(F32), (16, row_count)).astype(BF16)
        rank = dot(flags, upper.astype(F32).astype(BF16), 1, 0)[0:1, :].astype(jnp.int32)
        slot = jnp.where(inside, rank - 1, -1)
        pick = slot == lax.broadcasted_iota(jnp.int32, (per_shard, row_count), 0)
        picked_ref[...] = dot(pick.astype(F32).astype(BF16), v_ref[...], 1, 0)
        ids = jnp.sum(jnp.where(pick, lists, 0).astype(F32), axis=1, keepdims=True)
        ids_ref[...] = jnp.broadcast_to(ids.astype(jnp.int32), ids_ref.shape)
        acc_ref[...] = jnp.zeros_like(acc_ref)
        own_ref[...] = jnp.zeros_like(own_ref)

    ids = ids_ref[:, 0:1]
    here = ids == lax.broadcasted_iota(jnp.int32, (per_shard, chunk), 1) + step * chunk
    acc_ref[...] += dot(here.astype(F32).astype(BF16), c_ref[...], 1, 0)
    owner = jnp.where(here, owner_ref[...], 0).astype(F32)
    own_ref[...] += jnp.broadcast_to(jnp.sum(owner, axis=1, keepdims=True), own_ref.shape)

    @pl.when(step == pl.num_programs(0) - 1)
    def _():
        residual = (picked_ref[...] - acc_ref[...]).astype(BF16)
        r_ref[...] = dot(residual, rot_ref[...], 1, 0).astype(BF16)


def rotated_residuals(lists, v, centroids, owner, rotation, per_shard):
    row_count, width = v.shape
    total = centroids.shape[0]
    chunk = min(512, total)
    n = total // chunk
    fixed = lambda i: (0, 0)
    return pl.pallas_call(
        residual_kernel,
        grid=(n,),
        in_specs=[
            pl.BlockSpec((1, row_count), fixed),
            pl.BlockSpec((row_count, width), fixed),
            pl.BlockSpec((chunk, width), lambda i: (i, 0)),
            pl.BlockSpec((1, chunk), lambda i: (0, i)),
            pl.BlockSpec((width, width), fixed),
        ],
        out_specs=[
            pl.BlockSpec((per_shard, width), fixed),
            pl.BlockSpec((per_shard, 128), fixed),
        ],
        out_shape=[
            jax.ShapeDtypeStruct((per_shard, width), BF16),
            jax.ShapeDtypeStruct((per_shard, 128), F32),
        ],
        scratch_shapes=[
            pltpu.VMEM((per_shard, width), F32),
            pltpu.VMEM((per_shard, 128), jnp.int32),
            pltpu.VMEM((per_shard, width), F32),
        ],
        compiler_params=params(),
        cost_estimate=pl.CostEstimate(
            flops=2 * per_shard * width * (total + row_count + width),
            bytes_accessed=2 * total * width,
            transcendentals=0,
        ),
        name="residuals",
    )(lists, v, centroids, owner, rotation)


def moment_kernel(ids_ref, r_ref, own_ref, o_ref, *, sub):
    owners = o_ref.shape[0]
    rows, tile = r_ref.shape
    turned = r_ref[...].T
    own = own_ref[...].T[0:1, :]
    fold = tile // sub
    diagonal = (lax.broadcasted_iota(jnp.int32, (tile, tile), 0) // sub) == (
        lax.broadcasted_iota(jnp.int32, (tile, tile), 1) // sub
    )

    for place in range(owners):
        hit = own == ids_ref[place].astype(F32)
        masked = jnp.where(hit, turned.astype(F32), 0.0).astype(BF16)
        gram = jnp.where(diagonal, dot(masked, r_ref[...], 1, 0), 0.0)
        o_ref[place] = jnp.sum(gram.reshape(fold, sub, tile), axis=0)


def owner_moments(ids, rotated, own, sub):
    rows, width = rotated.shape
    owners = ids.shape[0]
    tile = 256 if width % 256 == 0 else width
    return pl.pallas_call(
        functools.partial(moment_kernel, sub=sub),
        grid_spec=pltpu.PrefetchScalarGridSpec(
            num_scalar_prefetch=1,
            grid=(width // tile,),
            in_specs=[
                pl.BlockSpec((rows, tile), lambda i, ids: (0, i)),
                pl.BlockSpec((rows, 128), lambda i, ids: (0, 0)),
            ],
            out_specs=pl.BlockSpec((owners, sub, tile), lambda i, ids: (0, 0, i)),
        ),
        out_shape=jax.ShapeDtypeStruct((owners, sub, width), F32),
        compiler_params=params(),
        cost_estimate=pl.CostEstimate(
            flops=2 * owners * rows * tile * width, bytes_accessed=4 * owners * sub * width, transcendentals=0
        ),
        name="moments",
    )(ids, rotated, own)


def flip(array, axis, mask):
    size = lax.axis_size(axis)
    return lax.ppermute(array, axis, [(i, i ^ mask) for i in range(size)])


def merge(a, b):
    top = jnp.maximum(a[0], b[0])
    return jnp.stack([top, a[1] * jnp.exp2(a[0] - top) + b[1] * jnp.exp2(b[0] - top)])


def reverse_bits(value, bits):
    return sum(((value >> k) & 1) << (bits - 1 - k) for k in range(bits))


def body(vectors, centroids, prior_mass, assign, owner_of, rotation):
    row_count, width = vectors.shape
    shard_rows = centroids.shape[0]
    cent_count, dp_count = lax.axis_size("cent"), lax.axis_size("dp")
    cent_pos, dp_pos = lax.axis_index("cent"), lax.axis_index("dp")
    bits = dp_count.bit_length() - 1
    levels = bits - 1
    block = shard_rows // dp_count
    scale = math.log2(math.e) / math.sqrt(width)

    half = dp_count // 4
    places = [1 + 2 * k for k in reversed(range(half))] + [2 * k for k in reversed(range(half))]
    ids = dp_pos ^ (2 * jnp.array(places, jnp.int32))
    c_blocks = centroids.reshape(dp_count, block, width)

    other = flip(vectors, "dp", 1)
    s1, st1 = scores_of(ids, vectors, c_blocks, scale)
    s2, st2 = scores_of(ids, other, c_blocks, scale)
    mine = jnp.concatenate([st1[0:2], st2[0:2]])
    theirs = flip(mine, "dp", 1)
    stats = jnp.concatenate([merge(mine[0:2], theirs[2:4]), merge(mine[2:4], theirs[0:2])])
    step = 1
    while step < cent_count:
        far = flip(stats, "cent", step)
        stats = jnp.concatenate([merge(stats[0:2], far[0:2]), merge(stats[2:4], far[2:4])])
        step *= 2
    stats = jnp.stack([stats[0], 1.0 / stats[1], stats[2], 1.0 / stats[3]])

    lists = jnp.where(assign // shard_rows == cent_pos, assign - cent_pos * shard_rows, -1)
    owner = lax.dynamic_slice_in_dim(owner_of, cent_pos * shard_rows, shard_rows, 0)
    rotated, own = rotated_residuals(
        lists[None], vectors, centroids, owner[None], rotation, row_count // cent_count
    )
    order = jnp.array([reverse_bits(k, bits) for k in range(dp_count)], jnp.int32)
    moments = owner_moments(dp_pos ^ order, rotated, own, width // M)

    parts, masses = {}, {}
    cuts = [(0, 1, BF16), (1, half - 1, BF16), (half, half, F32)]
    for first, n, kind in cuts:
        got, mass = sums_of(s1, s2, stats, vectors, other, first, n, kind)
        for k in range(n):
            parts[places[first + k]] = got[k]
            masses[places[first + k]] = mass[k]


    held = {}
    for place in places[:half]:
        held[place ^ 1] = parts[place ^ 1] + flip(parts[place], "dp", 2).astype(F32)
    for level in range(1, levels):
        bit = 1 << level
        sent = sorted((p for p in held if p & bit), reverse=True)
        for p in sent:
            came = flip(held.pop(p).astype(BF16), "dp", 2 * bit)
            held[p ^ bit] = held[p ^ bit] + came.astype(F32)
    own_sums = held[0]

    mass = jnp.concatenate([masses[reverse_bits(k, levels)] for k in range(2 * half)])
    for level in range(levels):
        n = mass.shape[0] // 2
        mass = mass[:n] + flip(mass[n:], "dp", 2 << level)
    own_mass = mass[0]

    n = dp_count // 2
    moments = moments[:n] + flip(moments[n:], "dp", 1)
    if cent_count == 2:
        near = width // 2
        mine = lax.dynamic_slice_in_dim(moments, cent_pos * near, near, 2)
        far = lax.dynamic_slice_in_dim(moments, (1 - cent_pos) * near, near, 2)
        moments = mine + flip(far, "cent", 1)
    else:
        moments = lax.psum_scatter(moments, "cent", scatter_dimension=2, tiled=True)
    for level in range(levels):
        n = moments.shape[0] // 2
        moments = moments[:n] + flip(moments[n:], "dp", 2 << level)
    moments = moments / row_count

    own_cent = lax.dynamic_slice_in_dim(centroids, dp_pos * block, block, 0).astype(F32)
    own_prior = lax.dynamic_slice_in_dim(prior_mass, dp_pos * block, block, 0)
    updated = (own_prior[:, None] * own_cent + own_sums) / (own_prior + own_mass)[:, None]
    return (updated[None], moments)


def solution(mesh):
    return jax.shard_map(
        body,
        mesh=mesh,
        in_specs=(P("dp", None), P("cent", None), P("cent"), P("dp"), P(), P()),
        out_specs=(P("cent", "dp", None), P("dp", None, "cent")),
        check_vma=False,
    )
```

time: 292 us -> 138 us (0.47)
  blocking collectives: 81.8 us -> 0 us
  Pallas kernels: 0 us -> 61.3 us
  waiting for transfers between devices: 95.2 us -> 36.3 us
  matrix products: 32.4 us -> 0 us
  other arithmetic: 34.4 us -> 11.7 us
  local copies, waits for them, and re-layouts: 24.6 us -> 7.23 us
  between operations: 14.8 us -> 0.79 us
  starting transfers between devices: 7.72 us -> 19.6 us
    unnamed x1 -> x0, blocking collectives: 73.1 us -> none
    reduce_scatter x2 -> x0, waiting for transfers between devices: 69.4 us -> none  [the longest x1 69.4 us: body(): lax.psum_scatter(sum_rows, 'dp', scatter_dimension=0, tiled=True)]
    pallas_call x0 -> x7, Pallas kernels: none -> 61.3 us  [the longest x2 22.5 us: scores_of(): pl.pallas_call(functools.partial(score_kernel, scale=scale), grid_spec=pl...]
    ppermute x0 -> x18, waiting for transfers between devices: none -> 36.3 us  [flip(): return lax.ppermute(array, axis, [(i, i ^ mask) for i in range(size)])]
    dot_general x4 -> x0, matrix products: 32.4 us -> none  [the longest x1 12.9 us: body(): lax.dot_general(member_prob, vectors, (((0,), (0,)), ((), ())), preferred...]
    all_to_all x1 -> x0, waiting for transfers between devices: 25.8 us -> none  [body(): lax.all_to_all(packed, 'dp', split_axis=0, concat_axis=0, tiled=True)]
    ppermute x0 -> x18, starting transfers between devices: none -> 19.6 us  [flip(): return lax.ppermute(array, axis, [(i, i ^ mask) for i in range(size)])]
    reduce_sum x4 -> x0, other arithmetic: 15.9 us -> none  [the longest x1 7.15 us: body(): soft_mass = jnp.sum(member_prob, axis=0, dtype=jnp.float32)]
  transfers between devices with their start and end apart: 3 -> 18, of which waited for: 2 -> 6; matrix products, arithmetic and copies ran while one was open for 14% -> 11% of each run, Pallas kernels for 0% -> 45%
where the time goes in v1:
time: 138 us; the launch traced here: 137 us
  Pallas kernels  61.3 us (44%)
  waiting for transfers between devices  36.3 us (26%)
  starting transfers between devices  19.6 us (14%)
  other arithmetic  11.7 us (8%)
  local copies, waits for them, and re-layouts  7.23 us (5%)
    ppermute x18, waiting for transfers between devices, flip(): return lax.ppermute(array, axis, [(i, i ^ mask) for i in range(size)])  36.3 us
    pallas_call x2, Pallas kernels, scores_of(): pl.pallas_call(functools.partial(score_kernel, scale=scale), grid_spec=pl...  22.5 us
    pallas_call x3, Pallas kernels, sums_of(): pl.pallas_call(sums_kernel, grid=(n,), in_specs=[score_spec, score_spec,...  19.7 us
    ppermute x18, starting transfers between devices, flip(): return lax.ppermute(array, axis, [(i, i ^ mask) for i in range(size)])  19.6 us
    pallas_call x1, Pallas kernels, rotated_residuals(): pl.pallas_call(residual_kernel, grid=(n,), in_specs=[pl.BlockSpec((1, row...  12.4 us
    pallas_call x1, Pallas kernels, owner_moments(): pl.pallas_call(functools.partial(moment_kernel, sub=sub), grid_spec=pltpu...  6.66 us
  transfers between devices with their start and end apart: 18, of which 6 were waited for; matrix products, arithmetic and copies ran while one was open for 11% of the time, Pallas kernels for 45%

profile of v1, /device:TPU:0, one launch (start us, length us, event | category | flops | bytes accessed | tf_op | source)
XLA Modules:
  0.0 136.8 jit_solution(681449431398644086)
XLA Ops:
  0.6 0.5 collective-permute-start
  1.1 1.3 subtract_select_fusion
  2.4 1.2 broadcast_xor_fusion.ids_ref
  3.7 1.3 dynamic_slice.17
  5.0 12.4 %residuals.1 = (bf16[512,768]{1,0:T(8,128)(2,1)}, f32[512,128]{1,0:T(8,128)}) custom-call(s32[1,1024]{1,0:T(1,128)} %bitcast.57, bf16[1024,768]{1,0:T(8,128)(2,1)} %v_ref.3, bf16[4096,768]{1,0:T(8,128)(2,1)} %c_ref.1, s32[1,4096]{1,0:T(1,128)} %bitcast.56, bf16[768,768]{1,0:T(8,128)(2,1)} %rot_ref.1), custom_call_target="tpu_custom_call" | custom-call | flops 4630511616 | bytes 6291456 | tf_op jit(solution)/shard_map/residuals/pallas_call | solution.py:166
  17.4 6.7 %moments.1 = f32[16,16,768]{2,1,0:T(8,128)} custom-call(s32[16]{0:T(128)} %broadcast_xor_fusion.ids_ref, bf16[512,768]{1,0:T(8,128)(2,1)} %get-tuple-element.24.r_ref, f32[512,128]{1,0:T(8,128)} %get-tuple-element.25.own_ref), custom_call_target="tpu_custom_call" | custom-call | flops 3221225472 | bytes 786432 | tf_op jit(solution)/shard_map/moments/pallas_call | solution.py:220
  24.0 1.0 slice.199
  25.1 0.1 collective-permute-start.13
  25.2 0.0 copy-done.3
  25.2 0.5 broadcast_xor_fusion.1.ids_ref
  25.7 1.2 collective-permute-done.13
  26.8 1.0 slice_add_fusion
  27.9 2.7 %collective-permute-start.14 = (f32[8,16,384]{2,1,0:T(8,128)S(1)}, f32[8,16,384]{2,1,0:T(8,128)S(1)}, u32[]{:S(2)}, u32[]{:S(2)}) collective-permute-start(f32[8,16,384]{2,1,0:T(8,128)S(1)} %constant_dynamic-slice_fusion), channel_id=1, source_target_pairs={{0,1},{1,0},{2,3},{3,2},{4,5},{5,4},{6,7},{7,6},{8,9},{9,8},{10,11... | collective-permute-start | bytes 589832 | tf_op jit(solution)/shard_map/ppermute | solution.py:242
  30.6 11.3 %scores.2 = (f32[8,256,1024]{2,1,0:T(8,128)}, f32[8,1024]{1,0:T(8,128)}) custom-call(s32[8]{0:T(128)} %broadcast_xor_fusion.1.ids_ref, bf16[1024,768]{1,0:T(8,128)(2,1)} %v_ref.3, bf16[16,256,768]{2,1,0:T(8,128)(2,1)} %bitcast.54), custom_call_target="tpu_custom_call" | custom-call | flops 3221225472 | bytes 8388608 | tf_op jit(solution)/shard_map/scores/pallas_call | solution.py:51
  41.9 0.8 slice.147
  42.7 0.0 collective-permute-done.14
  42.7 1.6 %collective-permute-start.15 = (f32[4,16,384]{2,1,0:T(8,128)S(1)}, f32[4,16,384]{2,1,0:T(8,128)S(1)}, u32[]{:S(2)}, u32[]{:S(2)}) collective-permute-start(f32[4,16,384]{2,1,0:T(8,128)S(1)} %slice.201), channel_id=1, source_target_pairs={{0,4},{2,6},{4,0},{6,2},{8,12},{10,14},{12,8},{14,10},{16,20},{18,... | collective-permute-start | bytes 294920 | tf_op jit(solution)/shard_map/ppermute | solution.py:242
  44.3 0.0 collective-permute-done.v_ref.v2_ref
  44.3 1.2 copy-done
  45.5 11.2 %scores.3 = (f32[8,256,1024]{2,1,0:T(8,128)}, f32[8,1024]{1,0:T(8,128)}) custom-call(s32[8]{0:T(128)} %broadcast_xor_fusion.1.ids_ref, bf16[1024,768]{1,0:T(8,128)(2,1)} %copy-done, bf16[16,256,768]{2,1,0:T(8,128)(2,1)} %bitcast.55), custom_call_target="tpu_custom_call" | custom-call | flops 3221225472 | bytes 8388608 | tf_op jit(solution)/shard_map/scores/pallas_call | solution.py:51
  56.7 0.8 slice.148
  57.5 0.1 collective-permute-start.1
  57.5 0.0 collective-permute-done.15
  57.6 1.6 %collective-permute-start.16 = (f32[2,16,384]{2,1,0:T(8,128)S(1)}, f32[2,16,384]{2,1,0:T(8,128)S(1)}, u32[]{:S(2)}, u32[]{:S(2)}) collective-permute-start(f32[2,16,384]{2,1,0:T(8,128)S(1)} %slice.203), channel_id=1, source_target_pairs={{0,8},{2,10},{4,12},{6,14},{8,0},{10,2},{12,4},{14,6},{16,24},{18,... | collective-permute-start | bytes 147464 | tf_op jit(solution)/shard_map/ppermute | solution.py:242
  59.2 0.0 collective-permute-done.1
  59.2 0.9 fusion.15
  60.2 0.6 collective-permute-start.2
  60.7 1.0 collective-permute-done.16
  61.8 2.7 %collective-permute-start.17 = (f32[1,16,384]{2,1,0:T(8,128)S(1)}, f32[1,16,384]{2,1,0:T(8,128)S(1)}, u32[]{:S(2)}, u32[]{:S(2)}) collective-permute-start(f32[1,16,384]{2,1,0:T(8,128)S(1)} %slice.205), channel_id=1, source_target_pairs={{0,16},{2,18},{4,20},{6,22},{8,24},{10,26},{12,28},{14,30},{16,0},... | collective-permute-start | bytes 73736 | tf_op jit(solution)/shard_map/ppermute | solution.py:242
  64.4 0.0 collective-permute-done.2
  64.5 0.6 pad_maximum_fusion.2.st_ref
  65.1 7.0 %sums.4 = (bf16[3,256,768]{2,1,0:T(8,128)(2,1)}, f32[3,1,256]{2,1,0:T(1,128)}) custom-call(f32[8,256,1024]{2,1,0:T(8,128)} %get-tuple-element.14.s1_ref, f32[8,256,1024]{2,1,0:T(8,128)} %get-tuple-element.15.s2_ref, f32[4,1024]{1,0:T(4,128)} %pad_maximum_fusion.2.st_ref, bf16[1024,768]{1,0:T(8,128)(2,1)} %v_ref.3, bf16[1024,768]{1,0:T(8,128)(2,1)} %copy-done), custom_call_target="tpu_custom_call" | custom-call | flops 2415919104 | bytes 6291456 | tf_op jit(solution)/shard_map/sums/pallas_call | solution.py:101
  72.1 1.3 slice_bitcast_fusion.2
  73.5 0.0 copy-start.2
  73.5 0.6 collective-permute-start.4
  74.1 4.3 %sums.5 = (bf16[1,256,768]{2,1,0:T(8,128)(2,1)}, f32[1,1,256]{2,1,0:T(1,128)}) custom-call(f32[8,256,1024]{2,1,0:T(8,128)} %get-tuple-element.14.s1_ref, f32[8,256,1024]{2,1,0:T(8,128)} %get-tuple-element.15.s2_ref, f32[4,1024]{1,0:T(4,128)} %pad_maximum_fusion.2.st_ref, bf16[1024,768]{1,0:T(8,128)(2,1)} %v_ref.3, bf16[1024,768]{1,0:T(8,128)(2,1)} %copy-done), custom_call_target="tpu_custom_call" | custom-call | flops 805306368 | bytes 2097152 | tf_op jit(solution)/shard_map/sums/pallas_call | solution.py:101
  78.3 1.5 %collective-permute-start.7 = (bf16[256,768]{1,0:T(8,128)(2,1)}, bf16[256,768]{1,0:T(8,128)(2,1)S(1)}, u32[]{:S(2)}, u32[]{:S(2)}) collective-permute-start(bf16[256,768]{1,0:T(8,128)(2,1)} %bitcast.60), channel_id=1, source_target_pairs={{0,4},{2,6},{4,0},{6,2},{8,12},{10,14},{12,8},{14,10},{16,20},{18,... | collective-permute-start | bytes 1179656 | tf_op jit(solution)/shard_map/ppermute | solution.py:242
  79.8 0.5 collective-permute-start.6
  80.4 0.7 pad_maximum_fusion.3
  81.1 1.6 %collective-permute-start.10 = (f32[4,256]{1,0:T(4,128)S(1)}, f32[4,256]{1,0:T(4,128)S(1)}, u32[]{:S(2)}, u32[]{:S(2)}) collective-permute-start(f32[4,256]{1,0:T(4,128)S(1)} %pad_maximum_fusion.3), channel_id=1, source_target_pairs={{0,4},{2,6},{4,0},{6,2},{8,12},{10,14},{12,8},{14,10},{16,20},{18,... | collective-permute-start | bytes 12296 | tf_op jit(solution)/shard_map/ppermute | solution.py:242
  82.6 8.4 %sums.3 = (f32[4,256,768]{2,1,0:T(8,128)}, f32[4,1,256]{2,1,0:T(1,128)}) custom-call(f32[8,256,1024]{2,1,0:T(8,128)} %get-tuple-element.14.s1_ref, f32[8,256,1024]{2,1,0:T(8,128)} %get-tuple-element.15.s2_ref, f32[4,1024]{1,0:T(4,128)} %pad_maximum_fusion.2.st_ref, bf16[1024,768]{1,0:T(8,128)(2,1)} %v_ref.3, bf16[1024,768]{1,0:T(8,128)(2,1)} %copy-done), custom_call_target="tpu_custom_call" | custom-call | flops 3221225472 | bytes 8388608 | tf_op jit(solution)/shard_map/sums/pallas_call | solution.py:101
  91.1 0.8 slice_bitcast_fusion.9
  91.9 9.0 %collective-permute-done.10 = f32[4,256]{1,0:T(4,128)S(1)} collective-permute-done((f32[4,256]{1,0:T(4,128)S(1)}, f32[4,256]{1,0:T(4,128)S(1)}, u32[]{:S(2)}, u32[]{:S(2)}) %collective-permute-start.10) | collective-permute-done | bytes 4128 | tf_op jit(solution)/shard_map/ppermute | solution.py:242
  100.9 1.6 %collective-permute-start.11 = (f32[2,256]{1,0:T(2,128)S(1)}, f32[2,256]{1,0:T(2,128)S(1)}, u32[]{:S(2)}, u32[]{:S(2)}) collective-permute-start(f32[2,256]{1,0:T(2,128)S(1)} %slice.195), channel_id=1, source_target_pairs={{0,8},{2,10},{4,12},{6,14},{8,0},{10,2},{12,4},{14,6},{16,24},{18,... | collective-permute-start | bytes 6152 | tf_op jit(solution)/shard_map/ppermute | solution.py:242
  102.6 0.0 collective-permute-done.4
  102.6 0.0 collective-permute-done.7
  102.6 1.5 %fusion.3 = (bf16[256,768]{1,0:T(8,128)(2,1)S(1)}, bf16[256,768]{1,0:T(8,128)(2,1)S(1)}) fusion(bf16[256,768]{1,0:T(8,128)(2,1)S(1)} %collective-permute-done.4, f32[4,256,768]{2,1,0:T(8,128)} %get-tuple-element.18, bf16[256,768]{1,0:T(8,128)(2,1)S(1)} %collective-permute-done.7), kind=kLoop, calls=%fused_computation.6 | loop fusion | flops 1179648 | bytes 3145728 | tf_op jit(solution)/shard_map/convert_element_type | solution.py:306
  104.1 0.5 collective-permute-start.8
  104.6 0.0 collective-permute-done.17
  104.6 0.6 fusion.9
  105.3 0.5 collective-permute-start.3
  105.8 0.0 collective-permute-done.11
  105.8 1.8 %collective-permute-start.12 = (f32[1,256]{1,0:T(1,128)S(1)}, f32[1,256]{1,0:T(1,128)S(1)}, u32[]{:S(2)}, u32[]{:S(2)}) collective-permute-start(f32[1,256]{1,0:T(1,128)S(1)} %slice.197), channel_id=1, source_target_pairs={{0,16},{2,18},{4,20},{6,22},{8,24},{10,26},{12,28},{14,30},{16,0},... | collective-permute-start | bytes 3080 | tf_op jit(solution)/shard_map/ppermute | solution.py:242
  107.6 1.0 collective-permute-start.5
  108.6 0.0 collective-permute-done.6
  108.6 11.8 %collective-permute-done.8 = bf16[256,768]{1,0:T(8,128)(2,1)S(1)} collective-permute-done((bf16[256,768]{1,0:T(8,128)(2,1)S(1)}, bf16[256,768]{1,0:T(8,128)(2,1)S(1)}, u32[]{:S(2)}, u32[]{:S(2)}) %collective-permute-start.8) | collective-permute-done | bytes 393248 | tf_op jit(solution)/shard_map/ppermute | solution.py:242
  120.5 0.1 fusion.2
  120.6 0.1 collective-permute-start.9
  120.7 0.0 collective-permute-done.12
  120.7 0.8 fusion.19
  121.5 0.0 collective-permute-done.3
  121.5 4.8 %collective-permute-done.5 = bf16[256,768]{1,0:T(8,128)(2,1)S(1)} collective-permute-done((bf16[256,768]{1,0:T(8,128)(2,1)S(1)}, bf16[256,768]{1,0:T(8,128)(2,1)S(1)}, u32[]{:S(2)}, u32[]{:S(2)}) %collective-permute-start.5) | collective-permute-done | bytes 393248 | tf_op jit(solution)/shard_map/ppermute | solution.py:242
  126.3 8.4 %collective-permute-done.9 = bf16[256,768]{1,0:T(8,128)(2,1)S(1)} collective-permute-done((bf16[256,768]{1,0:T(8,128)(2,1)S(1)}, bf16[256,768]{1,0:T(8,128)(2,1)S(1)}, u32[]{:S(2)}, u32[]{:S(2)}) %collective-permute-start.9) | collective-permute-done | bytes 393248 | tf_op jit(solution)/shard_map/ppermute | solution.py:242
  134.7 2.2 %fusion.8 = f32[1,256,768]{2,1,0:T(8,128)} fusion(bf16[256,768]{1,0:T(8,128)(2,1)S(1)} %collective-permute-done.9, bf16[256,768]{1,0:T(8,128)(2,1)S(1)} %collective-permute-done.5, bf16[256,768]{1,0:T(8,128)(2,1)S(1)} %collective-permute-done.3, f32[4,256,768]{2,1,0:T(8,128)S(1)} %copy-done.1, f32[256]{0:T(256)S(1)} %get-tuple-element.26, ...), kind=kLoop, calls=%fused_computation.12 | loop fusion | flops 1966080 | bytes 3147780 | tf_op jit(solution)/shard_map/broadcast_in_dim | solution.py:333
  (21 shorter events, 0.2 us)
Async XLA Ops:
  0.6 43.7 %collective-permute-start = (bf16[1024,768]{1,0:T(8,128)(2,1)}, bf16[1024,768]{1,0:T(8,128)(2,1)S(1)}, u32[]{:S(2)}, u32[]{:S(2)}) collective-permute-start(bf16[1024,768]{1,0:T(8,128)(2,1)} %v_ref.3), channel_id=1, source_target_pairs={{0,2},{2,0},{4,6},{6,4},{8,10},{10,8},{12,14},{14,12},{16,18},{18,... | collective-permute-start | bytes 4718600 | tf_op jit(solution)/shard_map/ppermute | solution.py:242
  17.4 7.8 %copy-start.3 = (s32[8]{0:T(128)S(1)}, s32[8]{0:T(128)}, u32[]{:S(2)}) copy-start(s32[8]{0:T(128)} %constant.51) | copy-start | bytes 100
  25.1 1.8 %collective-permute-start.13 = (f32[8,16,768]{2,1,0:T(8,128)S(1)}, f32[8,16,768]{2,1,0:T(8,128)S(1)}, u32[]{:S(2)}, u32[]{:S(2)}) collective-permute-start(f32[8,16,768]{2,1,0:T(8,128)S(1)} %slice.199), channel_id=1, source_target_pairs={{0,2},{2,0},{4,6},{6,4},{8,10},{10,8},{12,14},{14,12},{16,18},{18,... | collective-permute-start | bytes 1179656 | tf_op jit(solution)/shard_map/ppermute | solution.py:242
  27.9 14.8 %collective-permute-start.14 = (f32[8,16,384]{2,1,0:T(8,128)S(1)}, f32[8,16,384]{2,1,0:T(8,128)S(1)}, u32[]{:S(2)}, u32[]{:S(2)}) collective-permute-start(f32[8,16,384]{2,1,0:T(8,128)S(1)} %constant_dynamic-slice_fusion), channel_id=1, source_target_pairs={{0,1},{1,0},{2,3},{3,2},{4,5},{5,4},{6,7},{7,6},{8,9},{9,8},{10,11... | collective-permute-start | bytes 589832 | tf_op jit(solution)/shard_map/ppermute | solution.py:242
  42.7 14.8 %collective-permute-start.15 = (f32[4,16,384]{2,1,0:T(8,128)S(1)}, f32[4,16,384]{2,1,0:T(8,128)S(1)}, u32[]{:S(2)}, u32[]{:S(2)}) collective-permute-start(f32[4,16,384]{2,1,0:T(8,128)S(1)} %slice.201), channel_id=1, source_target_pairs={{0,4},{2,6},{4,0},{6,2},{8,12},{10,14},{12,8},{14,10},{16,20},{18,... | collective-permute-start | bytes 294920 | tf_op jit(solution)/shard_map/ppermute | solution.py:242
  44.3 1.2 copy-start
  57.5 1.8 %collective-permute-start.1 = (f32[4,1024]{1,0:T(4,128)S(1)}, f32[4,1024]{1,0:T(4,128)S(1)}, u32[]{:S(2)}, u32[]{:S(2)}) collective-permute-start(f32[4,1024]{1,0:T(4,128)S(1)} %pad_maximum_fusion), channel_id=1, source_target_pairs={{0,2},{2,0},{4,6},{6,4},{8,10},{10,8},{12,14},{14,12},{16,18},{18,... | collective-permute-start | bytes 49160 | tf_op jit(solution)/shard_map/ppermute | solution.py:242
  57.6 4.2 %collective-permute-start.16 = (f32[2,16,384]{2,1,0:T(8,128)S(1)}, f32[2,16,384]{2,1,0:T(8,128)S(1)}, u32[]{:S(2)}, u32[]{:S(2)}) collective-permute-start(f32[2,16,384]{2,1,0:T(8,128)S(1)} %slice.203), channel_id=1, source_target_pairs={{0,8},{2,10},{4,12},{6,14},{8,0},{10,2},{12,4},{14,6},{16,24},{18,... | collective-permute-start | bytes 147464 | tf_op jit(solution)/shard_map/ppermute | solution.py:242
  60.2 4.3 %collective-permute-start.2 = (f32[4,1024]{1,0:T(4,128)S(1)}, f32[4,1024]{1,0:T(4,128)S(1)}, u32[]{:S(2)}, u32[]{:S(2)}) collective-permute-start(f32[4,1024]{1,0:T(4,128)S(1)} %pad_maximum_fusion.1), channel_id=1, source_target_pairs={{0,1},{1,0},{2,3},{3,2},{4,5},{5,4},{6,7},{7,6},{8,9},{9,8},{10,11... | collective-permute-start | bytes 49160 | tf_op jit(solution)/shard_map/ppermute | solution.py:242
  61.8 42.9 %collective-permute-start.17 = (f32[1,16,384]{2,1,0:T(8,128)S(1)}, f32[1,16,384]{2,1,0:T(8,128)S(1)}, u32[]{:S(2)}, u32[]{:S(2)}) collective-permute-start(f32[1,16,384]{2,1,0:T(8,128)S(1)} %slice.205), channel_id=1, source_target_pairs={{0,16},{2,18},{4,20},{6,22},{8,24},{10,26},{12,28},{14,30},{16,0},... | collective-permute-start | bytes 73736 | tf_op jit(solution)/shard_map/ppermute | solution.py:242
  73.5 6.9 %copy-start.2 = (f32[3,1,256]{2,1,0:T(1,128)S(1)}, f32[3,1,256]{2,1,0:T(1,128)}, u32[]{:S(2)}) copy-start(f32[3,1,256]{2,1,0:T(1,128)} %get-tuple-element.22) | copy-start | bytes 9220
  73.5 29.1 %collective-permute-start.4 = (bf16[256,768]{1,0:T(8,128)(2,1)S(1)}, bf16[256,768]{1,0:T(8,128)(2,1)S(1)}, u32[]{:S(2)}, u32[]{:S(2)}) collective-permute-start(bf16[256,768]{1,0:T(8,128)(2,1)S(1)} %get-tuple-element.36), channel_id=1, source_target_pairs={{0,4},{2,6},{4,0},{6,2},{8,12},{10,14},{12,8},{14,10},{16,20},{18,... | collective-permute-start | bytes 1179656 | tf_op jit(solution)/shard_map/ppermute | solution.py:242
  78.3 24.2 %collective-permute-start.7 = (bf16[256,768]{1,0:T(8,128)(2,1)}, bf16[256,768]{1,0:T(8,128)(2,1)S(1)}, u32[]{:S(2)}, u32[]{:S(2)}) collective-permute-start(bf16[256,768]{1,0:T(8,128)(2,1)} %bitcast.60), channel_id=1, source_target_pairs={{0,4},{2,6},{4,0},{6,2},{8,12},{10,14},{12,8},{14,10},{16,20},{18,... | collective-permute-start | bytes 1179656 | tf_op jit(solution)/shard_map/ppermute | solution.py:242
  79.8 28.8 %collective-permute-start.6 = (bf16[256,768]{1,0:T(8,128)(2,1)S(1)}, bf16[256,768]{1,0:T(8,128)(2,1)S(1)}, u32[]{:S(2)}, u32[]{:S(2)}) collective-permute-start(bf16[256,768]{1,0:T(8,128)(2,1)S(1)} %get-tuple-element.35), channel_id=1, source_target_pairs={{0,4},{2,6},{4,0},{6,2},{8,12},{10,14},{12,8},{14,10},{16,20},{18,... | collective-permute-start | bytes 1179656 | tf_op jit(solution)/shard_map/ppermute | solution.py:242
  81.1 19.9 %collective-permute-start.10 = (f32[4,256]{1,0:T(4,128)S(1)}, f32[4,256]{1,0:T(4,128)S(1)}, u32[]{:S(2)}, u32[]{:S(2)}) collective-permute-start(f32[4,256]{1,0:T(4,128)S(1)} %pad_maximum_fusion.3), channel_id=1, source_target_pairs={{0,4},{2,6},{4,0},{6,2},{8,12},{10,14},{12,8},{14,10},{16,20},{18,... | collective-permute-start | bytes 12296 | tf_op jit(solution)/shard_map/ppermute | solution.py:242
  91.1 29.4 %copy-start.1 = (f32[4,256,768]{2,1,0:T(8,128)S(1)}, f32[4,256,768]{2,1,0:T(8,128)}, u32[]{:S(2)}) copy-start(f32[4,256,768]{2,1,0:T(8,128)} %get-tuple-element.18) | copy-start | bytes 9437188
  100.9 4.9 %collective-permute-start.11 = (f32[2,256]{1,0:T(2,128)S(1)}, f32[2,256]{1,0:T(2,128)S(1)}, u32[]{:S(2)}, u32[]{:S(2)}) collective-permute-start(f32[2,256]{1,0:T(2,128)S(1)} %slice.195), channel_id=1, source_target_pairs={{0,8},{2,10},{4,12},{6,14},{8,0},{10,2},{12,4},{14,6},{16,24},{18,... | collective-permute-start | bytes 6152 | tf_op jit(solution)/shard_map/ppermute | solution.py:242
  104.1 16.3 %collective-permute-start.8 = (bf16[256,768]{1,0:T(8,128)(2,1)S(1)}, bf16[256,768]{1,0:T(8,128)(2,1)S(1)}, u32[]{:S(2)}, u32[]{:S(2)}) collective-permute-start(bf16[256,768]{1,0:T(8,128)(2,1)S(1)} %get-tuple-element.33), channel_id=1, source_target_pairs={{0,8},{2,10},{4,12},{6,14},{8,0},{10,2},{12,4},{14,6},{16,24},{18,... | collective-permute-start | bytes 1179656 | tf_op jit(solution)/shard_map/ppermute | solution.py:242
  105.3 16.2 %collective-permute-start.3 = (bf16[256,768]{1,0:T(8,128)(2,1)S(1)}, bf16[256,768]{1,0:T(8,128)(2,1)S(1)}, u32[]{:S(2)}, u32[]{:S(2)}) collective-permute-start(bf16[256,768]{1,0:T(8,128)(2,1)S(1)} %get-tuple-element.34), channel_id=1, source_target_pairs={{0,4},{2,6},{4,0},{6,2},{8,12},{10,14},{12,8},{14,10},{16,20},{18,... | collective-permute-start | bytes 1179656 | tf_op jit(solution)/shard_map/ppermute | solution.py:242
  105.8 14.9 %collective-permute-start.12 = (f32[1,256]{1,0:T(1,128)S(1)}, f32[1,256]{1,0:T(1,128)S(1)}, u32[]{:S(2)}, u32[]{:S(2)}) collective-permute-start(f32[1,256]{1,0:T(1,128)S(1)} %slice.197), channel_id=1, source_target_pairs={{0,16},{2,18},{4,20},{6,22},{8,24},{10,26},{12,28},{14,30},{16,0},... | collective-permute-start | bytes 3080 | tf_op jit(solution)/shard_map/ppermute | solution.py:242
  107.6 18.7 %collective-permute-start.5 = (bf16[256,768]{1,0:T(8,128)(2,1)S(1)}, bf16[256,768]{1,0:T(8,128)(2,1)S(1)}, u32[]{:S(2)}, u32[]{:S(2)}) collective-permute-start(bf16[256,768]{1,0:T(8,128)(2,1)S(1)} %get-tuple-element.32), channel_id=1, source_target_pairs={{0,8},{2,10},{4,12},{6,14},{8,0},{10,2},{12,4},{14,6},{16,24},{18,... | collective-permute-start | bytes 1179656 | tf_op jit(solution)/shard_map/ppermute | solution.py:242
  120.6 14.1 %collective-permute-start.9 = (bf16[256,768]{1,0:T(8,128)(2,1)S(1)}, bf16[256,768]{1,0:T(8,128)(2,1)S(1)}, u32[]{:S(2)}, u32[]{:S(2)}) collective-permute-start(bf16[256,768]{1,0:T(8,128)(2,1)S(1)} %fusion.2), channel_id=1, source_target_pairs={{0,16},{2,18},{4,20},{6,22},{8,24},{10,26},{12,28},{14,30},{16,0},... | collective-permute-start | bytes 1179656 | tf_op jit(solution)/shard_map/ppermute | solution.py:242

commit v2 on v0

v2 whole, which is shorter than its diff:
```python
import functools
import math

import jax
import jax.numpy as jnp
from jax import lax
from jax.experimental import pallas as pl
from jax.experimental.pallas import tpu as pltpu
from jax.sharding import PartitionSpec as P

M = 48
CHUNK = 256
F32 = jnp.float32
BF16 = jnp.bfloat16
HBM = pl.BlockSpec(memory_space=pltpu.HBM)
VMEM = pl.BlockSpec(memory_space=pltpu.VMEM)
ANY = pl.BlockSpec(memory_space=pl.ANY)


def in_hbm(x):
    return pltpu.with_memory_space_constraint(x, pltpu.HBM)


def in_vmem(x):
    return pltpu.with_memory_space_constraint(x, pltpu.VMEM)


def params(mib):
    return pltpu.CompilerParams(vmem_limit_bytes=mib << 20)


def cost(flops, moved=0, exps=0):
    return pl.CostEstimate(flops=1024, bytes_accessed=1024, transcendentals=0)


def dot(a, b, ca, cb):
    return lax.dot_general(a, b, (((ca,), (cb,)), ((), ())), preferred_element_type=F32)


def reverse_bits(value, bits):
    return sum(((value >> k) & 1) << (bits - 1 - k) for k in range(bits))


def piece_order(levels, block):
    rest = levels - 3
    inner = [reverse_bits(k, rest) if rest else 0 for k in range(1 << rest)]
    order, pieces = [], {}
    for first, kind in ((1, "send"), (0, "keep")):
        for second, third in ((1, 1), (0, 1), (1, 0), (0, 0)):
            pieces[kind + str(second + 2 * third)] = (len(order) * block, len(inner) * block)
            order += [first + 2 * (second + 2 * third + 4 * k) for k in inner]
    return tuple(order), pieces


def swapped(place):
    return (place & ~3) | ((place & 1) << 1) | ((place >> 1) & 1)


def masks(level):
    return tuple(2 * p for p in ((1 << level), swapped(1 << level)))


def block_at(place, core):
    return lax.axis_index("dp") ^ jnp.where(core == 0, 2 * place, 2 * swapped(place))


def this_core():
    return lax.rem(lax.axis_index("dp"), 2)


def score_chunks(c_ref, v_ref, s_ref, scale, ready=None):
    def product(k):
        return dot(c_ref[k : k + CHUNK], v_ref[...], 1, 1)

    chunks = range(0, c_ref.shape[0], CHUNK)
    peak = None
    ahead = product(0)
    if ready is not None:
        ready()
    for place, k in enumerate(chunks):
        now = ahead
        if place + 1 < len(chunks):
            ahead = product(chunks[place + 1])
        c = c_ref[k : k + CHUNK].astype(F32)
        s = now * (2.0 * scale) - jnp.sum(c * c, axis=1, keepdims=True) * scale
        s_ref[k : k + CHUNK] = s
        top = jnp.max(s, axis=0, keepdims=True)
        if peak is None:
            peak, total = top, jnp.sum(jnp.exp2(s - top), axis=0, keepdims=True)
        else:
            top = jnp.maximum(peak, top)
            total = total * jnp.exp2(peak - top) + jnp.sum(jnp.exp2(s - top), axis=0, keepdims=True)
            peak = top
    return peak, total


def first_scores_kernel(v_ref, c_ref, s_ref, st_ref, ch_ref, vh_ref, v_sem, c_sem, *, places, scale):
    rows = ch_ref.shape[0] // len(places)
    core = this_core()
    copies = [
        pltpu.make_async_copy(c_ref.at[block_at(p, core)], ch_ref.at[pl.ds(k * rows, rows)], c_sem.at[k])
        for k, p in enumerate(places)
    ]
    whole = pltpu.make_async_copy(v_ref, vh_ref, v_sem)
    early = CHUNK // rows
    whole.start()
    for copy in copies:
        copy.start()
    for copy in copies[:early]:
        copy.wait()
    whole.wait()

    def rest():
        for copy in copies[early:]:
            copy.wait()

    peak, total = score_chunks(ch_ref, vh_ref, s_ref, scale, rest)
    st_ref[0:1, :] = peak
    st_ref[1:2, :] = total


def first_scores(v, c_blocks, places, scale):
    _, block, width = c_blocks.shape
    count, held = v.shape[0], len(places) * block
    return pl.pallas_call(
        functools.partial(first_scores_kernel, places=places, scale=scale),
        in_specs=[HBM, HBM],
        out_specs=[VMEM] * 4,
        out_shape=[
            pltpu.VMEM((held, count), F32),
            pltpu.VMEM((2, count), F32),
            pltpu.VMEM((held, width), BF16),
            pltpu.VMEM((count, width), BF16),
        ],
        scratch_shapes=[pltpu.SemaphoreType.DMA, pltpu.SemaphoreType.DMA((len(places),))],
        compiler_params=params(8),
        cost_estimate=cost(2 * held * width * count, 4 * held * width, held * count),
        name="first_scores",
    )(in_hbm(v), in_hbm(c_blocks))


def second_scores_kernel(v_ref, ch_ref, st_ref, s_ref, both_ref, *, scale):
    peak, total = score_chunks(ch_ref, v_ref, s_ref, scale)
    both_ref[0:2, :] = st_ref[...]
    both_ref[2:3, :] = peak
    both_ref[3:4, :] = total


def second_scores(v, c_half, stats, scale):
    held, width = c_half.shape
    count = v.shape[0]
    return pl.pallas_call(
        functools.partial(second_scores_kernel, scale=scale),
        in_specs=[VMEM, VMEM, VMEM],
        out_specs=[VMEM] * 2,
        out_shape=[pltpu.VMEM((held, count), F32), jax.ShapeDtypeStruct((4, count), F32)],
        compiler_params=params(8),
        cost_estimate=cost(2 * held * width * count, 0, held * count),
        name="second_scores",
    )(in_vmem(v), in_vmem(c_half), in_vmem(stats))


def merged(a, b):
    top = jnp.maximum(a[0], b[0])
    return top, a[1] * jnp.exp2(a[0] - top) + b[1] * jnp.exp2(b[0] - top)


def pair(ref, row):
    return ref[row : row + 1, :], ref[row + 1 : row + 2, :]


def merge_kernel(a_ref, b_ref, _, o_ref, *, swap):
    for row in (0, 2):
        top, total = merged(pair(a_ref, row), pair(b_ref, 2 - row if swap else row))
        o_ref[row : row + 1, :] = top
        o_ref[row + 1 : row + 2, :] = total


def merge(a, b, token, swap):
    return pl.pallas_call(
        functools.partial(merge_kernel, swap=swap),
        in_specs=[VMEM, VMEM, ANY],
        out_specs=VMEM,
        out_shape=jax.ShapeDtypeStruct(a.shape, F32),
        compiler_params=params(2),
        cost_estimate=cost(8 * a.size),
        name="merge",
    )(a, b, token)


def sums_kernel(s1_ref, s2_ref, near_ref, far_ref, v1_ref, v2_ref, old_ref, _, *refs, which, sends, rank):
    n = len(which)
    outs, mass_ref, sem = refs[:n], refs[n], refs[-1]
    stages = refs[n + 1 : n + 1 + sends] + outs[sends:]
    mass_ref[...] = old_ref[...]
    core = this_core()
    stats = []
    for row in (0, 2):
        top, total = merged(pair(near_ref, row), pair(far_ref, row))
        stats.append((top, 1.0 / total))

    def resp(k, size):
        rows = slice(k, k + size)
        return [
            (jnp.exp2(ref[rows, :] - top) * inverse).astype(BF16)
            for ref, (top, inverse) in zip((s1_ref, s2_ref), stats)
        ]

    work = [
        (place, k, start + k, min(CHUNK, size))
        for place, (start, size) in enumerate(which)
        for k in range(0, size, min(CHUNK, size))
    ]
    copies = []
    ahead = resp(work[0][2], work[0][3])
    for turn, (place, inside, k, step) in enumerate(work):
        r1, r2 = ahead
        if turn + 1 < len(work):
            ahead = resp(*work[turn + 1][2:])
        total = dot(r1, v1_ref[...], 1, 0) + dot(r2, v2_ref[...], 1, 0)
        stages[place][inside : inside + step] = total.astype(stages[place].dtype)
        both = r1.astype(F32) + r2.astype(F32)
        part = both[:, :128]
        for lane in range(128, both.shape[1], 128):
            part = part + both[:, lane : lane + 128]
        mass = jnp.sum(part.T, axis=0, keepdims=True)
        block = mass_ref.shape[1]
        for low in range(0, step, block):
            rows = rank[(k + low) // block]
            mass_ref[pl.ds(jnp.where(core == 0, *rows), 1), :] = mass[:, low : low + block]
        if inside + step == which[place][1] and place < sends:
            copy = pltpu.make_async_copy(stages[place], outs[place], sem.at[place])
            copy.start()
            copies.append(copy)
    for copy in copies:
        copy.wait()


def sums_of(s1, s2, near, far, v1, v2, old, which, sends, rank, token):
    count, width = v1.shape
    rows = [size for _, size in which]
    return pl.pallas_call(
        functools.partial(sums_kernel, which=which, sends=sends, rank=rank),
        in_specs=[VMEM] * 7 + [ANY],
        out_specs=[HBM] * sends + [VMEM] * (len(which) - sends + 1),
        out_shape=[pltpu.HBM((size, width), BF16) for size in rows[:sends]]
        + [pltpu.VMEM((size, width), F32) for size in rows[sends:]]
        + [jax.ShapeDtypeStruct(old.shape, F32)],
        scratch_shapes=[pltpu.VMEM((size, width), BF16) for size in rows[:sends]]
        + [pltpu.SemaphoreType.DMA((sends,))],
        compiler_params=params(14),
        cost_estimate=cost(0),
        name="sums",
    )(in_vmem(s1), in_vmem(s2), near, far, in_vmem(v1), in_vmem(v2), old, token)


def pick_kernel(assign_ref, v_ref, _, picked_ref, ids_ref, *, total):
    per_shard = picked_ref.shape[0]
    row_count = v_ref.shape[0]
    lists = assign_ref[...] - lax.axis_index("cent") * total
    inside = jnp.logical_and(lists >= 0, lists < total)
    upper = lax.broadcasted_iota(jnp.int32, (row_count, row_count), 0) <= (
        lax.broadcasted_iota(jnp.int32, (row_count, row_count), 1)
    )
    flags = jnp.broadcast_to(inside.astype(F32), (16, row_count)).astype(BF16)
    rank = dot(flags, upper.astype(F32).astype(BF16), 1, 0)[0:1, :].astype(jnp.int32)
    slot = jnp.where(inside, rank - 1, -1)
    pick = slot == lax.broadcasted_iota(jnp.int32, (per_shard, row_count), 0)
    picked_ref[...] = dot(pick.astype(F32).astype(BF16), v_ref[...], 1, 0).astype(BF16)
    ids = jnp.sum(jnp.where(pick, lists, 0).astype(F32), axis=1, keepdims=True)
    ids_ref[...] = jnp.broadcast_to(ids.astype(jnp.int32), ids_ref.shape)


def picked_rows(assign, v, token, per_shard, total):
    width = v.shape[1]
    return pl.pallas_call(
        functools.partial(pick_kernel, total=total),
        in_specs=[VMEM, VMEM, ANY],
        out_specs=[VMEM, VMEM],
        out_shape=[pltpu.VMEM((per_shard, width), BF16), pltpu.VMEM((per_shard, 128), jnp.int32)],
        compiler_params=params(8),
        cost_estimate=cost(0),
        name="picked",
    )(assign, in_vmem(v), token)


def residual_kernel(
    picked_ref, ids_ref, near_ref, c_ref, owner_ref, rot_ref, _, r_ref, own_ref, far_ref, sem, *, places
):
    held, width = near_ref.shape
    total = 2 * held
    block = held // len(places)
    per_shard = r_ref.shape[0]
    core, cent_pos = this_core(), lax.axis_index("cent")
    copies = [
        pltpu.make_async_copy(c_ref.at[block_at(p, core) ^ 1], far_ref.at[pl.ds(k * block, block)], sem.at[k])
        for k, p in enumerate(places)
    ]
    for copy in copies:
        copy.start()
    ids = ids_ref[:, 0:1]
    chunk = min(1024, held)
    lane_ids = lax.broadcasted_iota(jnp.int32, (1, chunk), 1)

    def one_hot(k, other):
        here_ids = lane_ids
        for low in range(0, chunk, block):
            first = (block_at(places[(k + low) // block], core) ^ other) * block
            in_block = jnp.logical_and(lane_ids >= low, lane_ids < low + block)
            here_ids = jnp.where(in_block, lane_ids - low + first, here_ids)
        return (ids == here_ids).astype(F32).astype(BF16)

    lists = ids + cent_pos * total
    high = (lists // 128 == lax.broadcasted_iota(jnp.int32, (1, owner_ref.shape[0]), 1)).astype(F32)
    table = dot(high.astype(BF16), owner_ref[...].astype(F32).astype(BF16), 1, 0)
    low = lists % 128 == lax.broadcasted_iota(jnp.int32, (1, 128), 1)
    own = jnp.sum(jnp.where(low, table, 0.0), axis=1, keepdims=True)
    own_ref[...] = jnp.broadcast_to(own, own_ref.shape)
    gathered = jnp.zeros((per_shard, width), F32)
    for other, half_ref in enumerate((near_ref, far_ref)):
        if other:
            for copy in copies:
                copy.wait()
        for k in range(0, held, chunk):
            gathered = gathered + dot(one_hot(k, other), half_ref[k : k + chunk], 1, 0)
    residual = (picked_ref[...].astype(F32) - gathered).astype(BF16)
    r_ref[...] = dot(residual, rot_ref[...], 1, 0).astype(BF16)


def rotated_residuals(picked, ids, c_half, c_blocks, owner, rotation, token, places):
    per_shard, width = picked.shape
    held = c_half.shape[0]
    return pl.pallas_call(
        functools.partial(residual_kernel, places=places),
        in_specs=[VMEM] * 3 + [HBM] + [VMEM] * 2 + [ANY],
        out_specs=[VMEM, VMEM],
        out_shape=[
            pltpu.VMEM((per_shard, width), BF16),
            pltpu.VMEM((per_shard, 128), F32),
        ],
        scratch_shapes=[pltpu.VMEM((held, width), BF16), pltpu.SemaphoreType.DMA((len(places),))],
        compiler_params=params(14),
        cost_estimate=cost(0),
        name="residuals",
    )(in_vmem(picked), in_vmem(ids), in_vmem(c_half), in_hbm(c_blocks), owner, rotation, token)


def moment_kernel(r_ref, own_ref, _, __, ___, keep_ref, send_ref, all_ref, *, sub, order):
    rows, width = r_ref.shape
    half = len(order)
    tile = 256 if width % 256 == 0 else width
    own = own_ref[...].T[0:1, :]
    diagonal = (lax.broadcasted_iota(jnp.int32, (tile, tile), 0) // sub) == (
        lax.broadcasted_iota(jnp.int32, (tile, tile), 1) // sub
    )
    dp_pos = lax.axis_index("dp")
    owners = [dp_pos ^ (2 * p) for p in order] + [dp_pos ^ (2 * p + 1) for p in order]
    hits = [(own == owner.astype(F32)).astype(F32).astype(BF16) for owner in owners]
    for t in range(0, width, tile):
        r = r_ref[:, t : t + tile]
        turned = r.T
        for place, hit in enumerate(hits):
            gram = jnp.where(diagonal, dot(turned * hit, r, 1, 0), 0.0)
            all_ref[place, :, t : t + tile] = jnp.sum(gram.reshape(tile // sub, sub, tile), axis=0)
    keep_ref[...] = all_ref[:half]
    send_ref[...] = all_ref[half:].astype(send_ref.dtype)


def owner_moments(order, rotated, own, token, s1, s2, sub):
    rows, width = rotated.shape
    half = len(order)
    shape = (half, sub, width)
    return pl.pallas_call(
        functools.partial(moment_kernel, sub=sub, order=order),
        in_specs=[VMEM, VMEM, ANY, VMEM, VMEM],
        out_specs=[VMEM] * 2,
        out_shape=[jax.ShapeDtypeStruct(shape, F32), jax.ShapeDtypeStruct(shape, BF16)],
        scratch_shapes=[pltpu.VMEM((2 * half, sub, width), F32)],
        compiler_params=params(8),
        cost_estimate=cost(0),
        name="moments",
    )(in_vmem(rotated), in_vmem(own), token, in_vmem(s1), in_vmem(s2))


def side_kernel(a_ref, b_ref, _, mine_ref, theirs_ref, all_ref):
    all_ref[...] = a_ref[...] + b_ref[...].astype(F32)
    size = mine_ref.shape[2]
    cent_pos = lax.axis_index("cent")
    for ref, side in ((mine_ref, cent_pos), (theirs_ref, 1 - cent_pos)):
        ref[...] = all_ref[:, :, pl.ds(pl.multiple_of(side * size, 128), size)]


def sides(a, b, token):
    n, sub, width = a.shape
    return pl.pallas_call(
        side_kernel,
        in_specs=[VMEM, VMEM, ANY],
        out_specs=[VMEM] * 2,
        out_shape=[jax.ShapeDtypeStruct((n, sub, width // 2), F32)] * 2,
        scratch_shapes=[pltpu.VMEM(a.shape, F32)],
        compiler_params=params(6),
        cost_estimate=cost(0),
        name="sides",
    )(a, b, token)


def pack_kernel(*refs, n):
    parts, mass_ref, outs = refs[:n], refs[n], refs[n + 2 :]
    total = parts[0][...]
    for part in parts[1:]:
        total = total + part[...]
    sub, width = total.shape[1:]
    block = mass_ref.shape[1]
    size = outs[0].shape[0]
    for k, ref in enumerate(outs):
        ref[:, :sub, :] = total[k * size : (k + 1) * size]
        ref[:, sub:, :] = jnp.zeros((size, ref.shape[1] - sub, width), F32)
        for place in range(size):
            row = k * size + place
            ref[place, sub : sub + 1, :block] = mass_ref[row : row + 1, :]


def packed(parts, mass, token):
    n, sub, width = parts[0].shape
    return pl.pallas_call(
        functools.partial(pack_kernel, n=len(parts)),
        in_specs=[VMEM] * (len(parts) + 1) + [ANY],
        out_specs=[VMEM] * 2,
        out_shape=[jax.ShapeDtypeStruct((n // 2, sub + 8, width), F32)] * 2,
        compiler_params=params(6),
        cost_estimate=cost(0),
        name="packed",
    )(*parts, mass, token)


def halves_kernel(*refs, n):
    total = refs[0][...]
    for part in refs[1:n]:
        total = total + part[...]
    size = total.shape[0] // 2
    refs[n + 1][...] = total[:size]
    refs[n + 2][...] = total[size:]


def halves(parts, token):
    n, rows, width = parts[0].shape
    return pl.pallas_call(
        functools.partial(halves_kernel, n=len(parts)),
        in_specs=[VMEM] * len(parts) + [ANY],
        out_specs=[VMEM] * 2,
        out_shape=[jax.ShapeDtypeStruct((n // 2, rows, width), F32)] * 2,
        compiler_params=params(4),
        cost_estimate=cost(0),
        name="halves",
    )(*parts, token)


def flip(array, axis, mask):
    size = lax.axis_size(axis)
    return lax.ppermute(array, axis, [(i, i ^ mask) for i in range(size)])


def exchange(array, level):
    size, far = lax.axis_size("dp"), masks(level)
    return lax.ppermute(array, "dp", [(i, i ^ far[i % 2]) for i in range(size)])


def joined(a, b):
    return a + b.astype(F32)


def add_kernel(*refs, starts, rows):
    parts = refs[: len(starts)]
    o_ref, stage, sem = refs[-3:]
    total = parts[0][starts[0] : starts[0] + rows].astype(F32)
    for part, start in zip(parts[1:], starts[1:]):
        total = total + part[start : start + rows].astype(F32)
    stage[...] = total.astype(stage.dtype)
    copy = pltpu.make_async_copy(stage, o_ref, sem)
    copy.start()
    copy.wait()


def added(parts, starts, rows, *tokens):
    shape = (rows, parts[0].shape[1])
    return pl.pallas_call(
        functools.partial(add_kernel, starts=starts, rows=rows),
        in_specs=[VMEM] * len(parts) + [ANY] * len(tokens),
        out_specs=HBM,
        out_shape=pltpu.HBM(shape, BF16),
        scratch_shapes=[pltpu.VMEM(shape, BF16), pltpu.SemaphoreType.DMA],
        compiler_params=params(6),
        cost_estimate=cost(0),
        name="added",
    )(*parts, *tokens)


def update_kernel(c_ref, prior_ref, small_ref, more_ref, *refs, count, parts):
    o_ref, moment_ref = refs[-2:]
    rows = o_ref.shape[0]
    sub = moment_ref.shape[1]
    small = small_ref[0] + more_ref[0]
    moment_ref[0] = small[:sub] * (1.0 / count)
    prior = prior_ref[...]
    inverse = 1.0 / (prior + small[sub : sub + 1, :rows])
    columns = jnp.concatenate([prior, inverse, jnp.zeros((6, rows), F32)], axis=0).T
    start = 0
    for k, n in enumerate(parts):
        total = refs[0][...].astype(F32)
        for ref in refs[1:n]:
            total = total + ref[...].astype(F32)
        refs = refs[n:]
        here = slice(start, start + total.shape[0])
        start += total.shape[0]
        o_ref[here] = (columns[here, 0:1] * c_ref[here].astype(F32) + total) * columns[here, 1:2]


def body(vectors, centroids, prior_mass, assign, owner_of, rotation):
    row_count, width = vectors.shape
    shard_rows = centroids.shape[0]
    cent_count, dp_count = lax.axis_size("cent"), lax.axis_size("dp")
    cent_pos, dp_pos = lax.axis_index("cent"), lax.axis_index("dp")
    bits = dp_count.bit_length() - 1
    levels = bits - 1
    block = shard_rows // dp_count
    scale = math.log2(math.e) / math.sqrt(width)
    own_cent = lax.dynamic_slice_in_dim(centroids, dp_pos * block, block, 0)
    own_prior = lax.dynamic_slice_in_dim(prior_mass, dp_pos * block, block, 0)

    places, at = piece_order(levels, block)
    c_blocks = centroids.reshape(dp_count, block, width)
    other = flip(vectors, "dp", 1)
    s1, stats, c_half, v1 = first_scores(vectors, c_blocks, places, scale)
    s2, near = second_scores(other, c_half, stats, scale)
    picked, ids = picked_rows(assign[None], v1, near, row_count // cent_count, shard_rows)
    near = merge(near, flip(near, "dp", 1), ids, True)
    step = 1
    while 2 * step < cent_count:
        near = merge(near, flip(near, "cent", step), ids, False)
        step *= 2
    far = flip(near, "cent", step)

    rotated, own = rotated_residuals(
        picked, ids, c_half, c_blocks, owner_of.reshape(-1, 128), rotation, near, places
    )

    rank = tuple((reverse_bits(p, levels), reverse_bits(swapped(p), levels)) for p in places)
    step_args = (s1, s2, near, far, v1, other)
    blank = jnp.zeros((dp_count // 2, block), F32)

    def sums(mass, names, token):
        sends = sum(name.startswith("send") for name in names)
        return sums_of(*step_args, mass, tuple(at[name] for name in names), sends, rank, token)

    got3, mass = sums(blank, ("send3",), own)
    came3 = exchange(got3, 0)

    order = [reverse_bits(k, levels) for k in range(1 << levels)]
    keep, sent = owner_moments(order, rotated, own, mass, s1, s2, width // M)
    sent = flip(sent, "dp", 1)
    got2, kept3, kept2, mass = sums(mass, ("send2", "keep3", "keep2"), keep)
    came2 = exchange(got2, 0)
    n = kept3.shape[0]
    next3 = added([kept3, came3], [0, 0], n, mass)
    over3 = exchange(next3, 1)
    if cent_count == 2:
        keep, sent = sides(keep, sent, in_hbm(next3))
        moments = [keep, flip(sent, "cent", 1)]
    else:
        moments = [lax.psum_scatter(joined(keep, sent), "cent", scatter_dimension=2, tiled=True)]
    got1, got0, kept1, kept0, mass = sums(mass, ("send1", "send0", "keep1", "keep0"), keep)
    came1, came0 = exchange(got1, 0), exchange(got0, 0)
    next2 = added([kept2, came2, over3], [0, 0, 0], n, kept0)
    over2 = exchange(next2, 2)

    keep, sent = packed(moments, mass, in_hbm(next2))
    small = [keep, flip(sent, "dp", 2)]
    next1 = added([kept1, came1], [0, 0], n, keep)
    over1 = exchange(next1, 1)
    token = in_hbm(next1)
    for level in range(1, levels):
        keep, sent = halves(small, token)
        small = [keep, flip(sent, "dp", 2 << level)]
        token = keep
    parts = [[kept0, came0, over1, over2]]
    level = 3
    while level < levels:
        total = jnp.concatenate([sum(p.astype(F32) for p in part) for part in parts])
        n = total.shape[0] // 2
        parts = [[total[:n], exchange(total[n:].astype(BF16), level)]]
        level += 1
    sub, near_half = width // M, width // cent_count
    updated, moments = pl.pallas_call(
        functools.partial(update_kernel, count=row_count, parts=tuple(len(part) for part in parts)),
        in_specs=[VMEM] * (4 + sum(len(part) for part in parts)),
        out_specs=[VMEM] * 2,
        out_shape=[
            jax.ShapeDtypeStruct((block, width), F32),
            jax.ShapeDtypeStruct((1, sub, near_half), F32),
        ],
        compiler_params=params(4),
        cost_estimate=cost(8 * block * width),
        name="update",
    )(own_cent, own_prior[None], *small, *(p for part in parts for p in part))
    return (updated[None], moments)


def solution(mesh):
    return jax.shard_map(
        body,
        mesh=mesh,
        in_specs=(P("dp", None), P("cent", None), P("cent"), P("dp"), P(), P()),
        out_specs=(P("cent", "dp", None), P("dp", None, "cent")),
        check_vma=False,
    )
```

time: 292 us -> 74.8 us (0.26)
  blocking collectives: 81.8 us -> 0 us
  waiting for transfers between devices: 95.2 us -> 17.6 us
  Pallas kernels: 0 us -> 36 us
  other arithmetic: 34.4 us -> 0 us
  matrix products: 32.4 us -> 0 us
  local copies, waits for them, and re-layouts: 24.6 us -> 1.81 us
  between operations: 14.8 us -> 0.81 us
  starting transfers between devices: 7.72 us -> 18.4 us
    unnamed x1 -> x0, blocking collectives: 73.1 us -> none
    reduce_scatter x2 -> x0, waiting for transfers between devices: 69.4 us -> none  [the longest x1 69.4 us: body(): lax.psum_scatter(sum_rows, 'dp', scatter_dimension=0, tiled=True)]
    pallas_call x0 -> x17, Pallas kernels: none -> 36 us  [the longest x3 8.75 us: sums_of(): pl.pallas_call(functools.partial(sums_kernel, which=which, sends=sends, r...]
    dot_general x4 -> x0, matrix products: 32.4 us -> none  [the longest x1 12.9 us: body(): lax.dot_general(member_prob, vectors, (((0,), (0,)), ((), ())), preferred...]
    all_to_all x1 -> x0, waiting for transfers between devices: 25.8 us -> none  [body(): lax.all_to_all(packed, 'dp', split_axis=0, concat_axis=0, tiled=True)]
    ppermute x0 -> x15, starting transfers between devices: none -> 18.4 us  [the longest x7 10.1 us: exchange(): return lax.ppermute(array, 'dp', [(i, i ^ far[i % 2]) for i in range(size)])]
    ppermute x0 -> x15, waiting for transfers between devices: none -> 17.6 us  [the longest x8 12.4 us: flip(): return lax.ppermute(array, axis, [(i, i ^ mask) for i in range(size)])]
    reduce_sum x4 -> x0, other arithmetic: 15.9 us -> none  [the longest x1 7.15 us: body(): soft_mass = jnp.sum(member_prob, axis=0, dtype=jnp.float32)]
  transfers between devices with their start and end apart: 3 -> 15, of which waited for: 2 -> 7; matrix products, arithmetic and copies ran while one was open for 14% -> 2% of each run, Pallas kernels for 0% -> 39%
where the time goes in v2:
time: 74.8 us; the launch traced here: 74.6 us
  Pallas kernels  36 us (48%)
  starting transfers between devices  18.4 us (25%)
  waiting for transfers between devices  17.6 us (24%)
  local copies, waits for them, and re-layouts  1.81 us (2%)
  between operations  0.81 us (1%)
    ppermute x8, waiting for transfers between devices, flip(): return lax.ppermute(array, axis, [(i, i ^ mask) for i in range(size)])  12.4 us
    ppermute x7, starting transfers between devices, exchange(): return lax.ppermute(array, 'dp', [(i, i ^ far[i % 2]) for i in range(size)])  10.1 us
    pallas_call x3, Pallas kernels, sums_of(): pl.pallas_call(functools.partial(sums_kernel, which=which, sends=sends, r...  8.75 us
    ppermute x8, starting transfers between devices, flip(): return lax.ppermute(array, axis, [(i, i ^ mask) for i in range(size)])  8.27 us
    pallas_call x1, Pallas kernels, rotated_residuals(): pl.pallas_call(functools.partial(residual_kernel, places=places), in_spec...  7.01 us
    pallas_call x1, Pallas kernels, first_scores(): pl.pallas_call(functools.partial(first_scores_kernel, places=places, scal...  6.9 us
    ppermute x7, waiting for transfers between devices, exchange(): return lax.ppermute(array, 'dp', [(i, i ^ far[i % 2]) for i in range(size)])  5.23 us
    pallas_call x1, Pallas kernels, second_scores(): pl.pallas_call(functools.partial(second_scores_kernel, scale=scale), in_s...  4.2 us
  transfers between devices with their start and end apart: 15, of which 7 were waited for; matrix products, arithmetic and copies ran while one was open for 2% of the time, Pallas kernels for 39%

profile of v2, /device:TPU:0, one launch (start us, length us, event | category | flops | bytes accessed | tf_op | source)
XLA Modules:
  0.0 74.6 jit_solution(301430714409200960)
XLA Ops:
  0.6 0.5 collective-permute-start
  1.1 6.9 %first_scores.1 = (f32[2048,1024]{1,0:T(8,128)S(1)}, f32[2,1024]{1,0:T(2,128)S(1)}, bf16[2048,768]{1,0:T(8,128)(2,1)S(1)}, bf16[1024,768]{1,0:T(8,128)(2,1)S(1)}) custom-call(bf16[1024,768]{1,0:T(8,128)(2,1)} %v_ref.1, bf16[16,256,768]{2,1,0:T(8,128)(2,1)} %bitcast.8), custom_call_target="tpu_custom_call" | custom-call | flops 1024 | bytes 1024 | tf_op jit(solution)/shard_map/first_scores/pallas_call | solution.py:125
  8.1 0.0 copy-start.2
  8.1 0.0 collective-permute-done.v_ref.v2_ref
  8.1 0.0 copy-start
  8.1 0.0 copy-start.1
  8.1 4.2 %second_scores.1 = (f32[2048,1024]{1,0:T(8,128)S(1)}, f32[4,1024]{1,0:T(4,128)S(1)}) custom-call(bf16[1024,768]{1,0:T(8,128)(2,1)S(1)} %collective-permute-done.v_ref.v2_ref, bf16[2048,768]{1,0:T(8,128)(2,1)S(1)} %get-tuple-element.36.ch_ref.near_ref, f32[2,1024]{1,0:T(2,128)S(1)} %get-tuple-element.37.st_ref), custom_call_target="tpu_custom_call" | custom-call | flops 1024 | bytes 1024 | tf_op jit(solution)/shard_map/second_scores/pallas_call | solution.py:152
  12.3 0.1 collective-permute-start.1
  12.4 0.0 copy-done.2
  12.4 1.6 %picked.1 = (bf16[512,768]{1,0:T(8,128)(2,1)S(1)}, s32[512,128]{1,0:T(8,128)S(1)}) custom-call(s32[1,1024]{1,0:T(1,128)S(1)} %bitcast.6, bf16[1024,768]{1,0:T(8,128)(2,1)S(1)} %get-tuple-element.35.v_ref.v1_ref, f32[4,1024]{1,0:T(4,128)S(1)} %get-tuple-element.38._.a_ref), custom_call_target="tpu_custom_call" | custom-call | flops 1024 | bytes 1024 | tf_op jit(solution)/shard_map/picked/pallas_call | solution.py:276
  14.0 0.0 collective-permute-done.1.b_ref
  14.0 3.0 %collective-permute-start.2 = (f32[4,1024]{1,0:T(4,128)S(1)}, f32[4,1024]{1,0:T(4,128)S(1)}, u32[]{:S(2)}, u32[]{:S(2)}) collective-permute-start(f32[4,1024]{1,0:T(4,128)S(1)} %merge.1._.near_ref), channel_id=1, source_target_pairs={{0,1},{1,0},{2,3},{3,2},{4,5},{5,4},{6,7},{7,6},{8,9},{9,8},{10,11... | collective-permute-start | bytes 49160 | tf_op jit(solution)/shard_map/ppermute | solution.py:460
  17.1 0.0 copy-done
  17.1 0.0 copy-done.1
  17.1 7.0 %residuals.1 = (bf16[512,768]{1,0:T(8,128)(2,1)S(1)}, f32[512,128]{1,0:T(8,128)S(1)}) custom-call(bf16[512,768]{1,0:T(8,128)(2,1)S(1)} %get-tuple-element.39.picked_ref, s32[512,128]{1,0:T(8,128)S(1)} %get-tuple-element.40._.ids_ref, bf16[2048,768]{1,0:T(8,128)(2,1)S(1)} %get-tuple-element.36.ch_ref.near_ref, bf16[16,256,768]{2,1,0:T(8,128)(2,1)} %bitcast.9, ...), custom_call_target="tpu_custom_call" | custom-call | flops 1024 | bytes 1024 | tf_op jit(solution)/shard_map/residuals/pallas_call | solution.py:333
  24.1 0.0 collective-permute-done.2.far_ref
  24.1 1.7 %sums.3 = (bf16[256,768]{1,0:T(8,128)(2,1)}, f32[8,256]{1,0:T(8,128)S(1)}) custom-call(f32[2048,1024]{1,0:T(8,128)S(1)} %get-tuple-element.43.s1_ref.__, f32[2048,1024]{1,0:T(8,128)S(1)} %get-tuple-element.44.s2_ref.___, f32[4,1024]{1,0:T(4,128)S(1)} %merge.1._.near_ref, f32[4,1024]{1,0:T(4,128)S(1)} %collective-permute-done.2.far_ref, ...), custom_call_target="tpu_custom_call" | custom-call | flops 1024 | bytes 1024 | tf_op jit(solution)/shard_map/sums/pallas_call | solution.py:242
  25.8 1.6 %collective-permute-start.4 = (bf16[256,768]{1,0:T(8,128)(2,1)}, bf16[256,768]{1,0:T(8,128)(2,1)S(1)}, u32[]{:S(2)}, u32[]{:S(2)}) collective-permute-start(bf16[256,768]{1,0:T(8,128)(2,1)} %get-tuple-element.49), channel_id=1, source_target_pairs={{0,4},{2,10},{4,0},{6,14},{8,12},{10,2},{12,8},{14,6},{16,20},{18,... | collective-permute-start | bytes 1179656 | tf_op jit(solution)/shard_map/ppermute | solution.py:465
  27.4 3.6 %moments.1 = (f32[8,16,768]{2,1,0:T(8,128)S(1)}, bf16[8,16,768]{2,1,0:T(8,128)(2,1)S(1)}) custom-call(bf16[512,768]{1,0:T(8,128)(2,1)S(1)} %get-tuple-element.41.r_ref, f32[512,128]{1,0:T(8,128)S(1)} %get-tuple-element.42._.own_ref, f32[8,256]{1,0:T(8,128)S(1)} %get-tuple-element.45._.old_ref, f32[2048,1024]{1,0:T(8,128)S(1)} %get-tuple-element.43.s1_ref.__, ...), custom_call_target="tpu_custom_call" | custom-call | flops 1024 | bytes 1024 | tf_op jit(solution)/shard_map/moments/pallas_call | solution.py:373
  31.0 0.1 collective-permute-start.3
  31.0 2.8 %sums.4 = (bf16[256,768]{1,0:T(8,128)(2,1)}, f32[256,768]{1,0:T(8,128)S(1)}, f32[256,768]{1,0:T(8,128)S(1)}, f32[8,256]{1,0:T(8,128)S(1)}) custom-call(f32[2048,1024]{1,0:T(8,128)S(1)} %get-tuple-element.43.s1_ref.__, f32[2048,1024]{1,0:T(8,128)S(1)} %get-tuple-element.44.s2_ref.___, f32[4,1024]{1,0:T(4,128)S(1)} %merge.1._.near_ref, ...), custom_call_target="tpu_custom_call" | custom-call | flops 1024 | bytes 1024 | tf_op jit(solution)/shard_map/sums/pallas_call | solution.py:242
  33.9 1.1 %collective-permute-start.6 = (bf16[256,768]{1,0:T(8,128)(2,1)}, bf16[256,768]{1,0:T(8,128)(2,1)S(1)}, u32[]{:S(2)}, u32[]{:S(2)}) collective-permute-start(bf16[256,768]{1,0:T(8,128)(2,1)} %get-tuple-element.55), channel_id=1, source_target_pairs={{0,4},{2,10},{4,0},{6,14},{8,12},{10,2},{12,8},{14,6},{16,20},{18,... | collective-permute-start | bytes 1179656 | tf_op jit(solution)/shard_map/ppermute | solution.py:465
  35.0 0.0 collective-permute-done.4.refs_1_
  35.0 0.8 %added.3._ = bf16[256,768]{1,0:T(8,128)(2,1)} custom-call(f32[256,768]{1,0:T(8,128)S(1)} %get-tuple-element.48.refs_0_, bf16[256,768]{1,0:T(8,128)(2,1)S(1)} %collective-permute-done.4.refs_1_, f32[8,256]{1,0:T(8,128)S(1)} %get-tuple-element.50.refs_2_.old_ref), custom_call_target="tpu_custom_call" | custom-call | flops 1024 | bytes 1024 | tf_op jit(solution)/shard_map/added/pallas_call | solution.py:486
  35.8 1.1 %collective-permute-start.7 = (bf16[256,768]{1,0:T(8,128)(2,1)}, bf16[256,768]{1,0:T(8,128)(2,1)S(1)}, u32[]{:S(2)}, u32[]{:S(2)}) collective-permute-start(bf16[256,768]{1,0:T(8,128)(2,1)} %added.3._), channel_id=1, source_target_pairs={{0,8},{2,6},{4,12},{6,2},{8,0},{10,14},{12,4},{14,10},{16,24},{18,... | collective-permute-start | bytes 1179656 | tf_op jit(solution)/shard_map/ppermute | solution.py:465
  37.0 0.0 collective-permute-done.3.b_ref
  37.0 0.1 sides.1
  37.1 4.2 %sums.5 = (bf16[256,768]{1,0:T(8,128)(2,1)}, bf16[256,768]{1,0:T(8,128)(2,1)}, f32[256,768]{1,0:T(8,128)S(1)}, f32[256,768]{1,0:T(8,128)S(1)}, f32[8,256]{1,0:T(8,128)S(1)}) custom-call(f32[2048,1024]{1,0:T(8,128)S(1)} %get-tuple-element.43.s1_ref.__, f32[2048,1024]{1,0:T(8,128)S(1)} %get-tuple-element.44.s2_ref.___, f32[4,1024]{1,0:T(4,128)S(1)} %merge.1._.near_ref, ...), custom_call_target="tpu_custom_call" | custom-call | flops 1024 | bytes 1024 | tf_op jit(solution)/shard_map/sums/pallas_call | solution.py:242
  41.2 1.6 %collective-permute-start.9 = (bf16[256,768]{1,0:T(8,128)(2,1)}, bf16[256,768]{1,0:T(8,128)(2,1)S(1)}, u32[]{:S(2)}, u32[]{:S(2)}) collective-permute-start(bf16[256,768]{1,0:T(8,128)(2,1)} %get-tuple-element.60), channel_id=1, source_target_pairs={{0,4},{2,10},{4,0},{6,14},{8,12},{10,2},{12,8},{14,6},{16,20},{18,... | collective-permute-start | bytes 1179656 | tf_op jit(solution)/shard_map/ppermute | solution.py:465
  42.8 0.5 collective-permute-start.5
  43.3 0.5 collective-permute-start.12
  43.8 0.5 collective-permute-done.6.refs_1_
  44.4 2.9 %collective-permute-done.7.refs_2_ = bf16[256,768]{1,0:T(8,128)(2,1)S(1)} collective-permute-done((bf16[256,768]{1,0:T(8,128)(2,1)}, bf16[256,768]{1,0:T(8,128)(2,1)S(1)}, u32[]{:S(2)}, u32[]{:S(2)}) %collective-permute-start.7) | collective-permute-done | bytes 393248 | tf_op jit(solution)/shard_map/ppermute | solution.py:465
  47.2 0.9 %added.4.refs_3_ = bf16[256,768]{1,0:T(8,128)(2,1)} custom-call(f32[256,768]{1,0:T(8,128)S(1)} %get-tuple-element.54.refs_0_, bf16[256,768]{1,0:T(8,128)(2,1)S(1)} %collective-permute-done.6.refs_1_, bf16[256,768]{1,0:T(8,128)(2,1)S(1)} %collective-permute-done.7.refs_2_, f32[256,768]{1,0:T(8,128)S(1)} %get-tuple-element.56.refs_3_.refs_0_), custom_call_target="tpu_custom_call" | custom-call | flops 1024 | bytes 1024 | tf_op jit(solution)/shard_map/added/pallas_call | solution.py:486
  48.1 0.4 collective-permute-done.5.refs_1_
  48.5 1.8 %collective-permute-done.9.refs_1_ = bf16[256,768]{1,0:T(8,128)(2,1)S(1)} collective-permute-done((bf16[256,768]{1,0:T(8,128)(2,1)}, bf16[256,768]{1,0:T(8,128)(2,1)S(1)}, u32[]{:S(2)}, u32[]{:S(2)}) %collective-permute-start.9) | collective-permute-done | bytes 393248 | tf_op jit(solution)/shard_map/ppermute | solution.py:465
  50.4 0.8 %added.5.refs_2_ = bf16[256,768]{1,0:T(8,128)(2,1)} custom-call(f32[256,768]{1,0:T(8,128)S(1)} %get-tuple-element.59.refs_0_, bf16[256,768]{1,0:T(8,128)(2,1)S(1)} %collective-permute-done.9.refs_1_, f32[4,24,384]{2,1,0:T(8,128)S(1)} %get-tuple-element.57.refs_2_.refs_0_), custom_call_target="tpu_custom_call" | custom-call | flops 1024 | bytes 1024 | tf_op jit(solution)/shard_map/added/pallas_call | solution.py:486
  51.2 1.7 %collective-permute-start.13 = (bf16[256,768]{1,0:T(8,128)(2,1)}, bf16[256,768]{1,0:T(8,128)(2,1)S(1)}, u32[]{:S(2)}, u32[]{:S(2)}) collective-permute-start(bf16[256,768]{1,0:T(8,128)(2,1)} %added.5.refs_2_), channel_id=1, source_target_pairs={{0,8},{2,6},{4,12},{6,2},{8,0},{10,14},{12,4},{14,10},{16,24},{18,... | collective-permute-start | bytes 1179656 | tf_op jit(solution)/shard_map/ppermute | solution.py:465
  52.9 2.6 %collective-permute-start.14 = (bf16[256,768]{1,0:T(8,128)(2,1)}, bf16[256,768]{1,0:T(8,128)(2,1)S(1)}, u32[]{:S(2)}, u32[]{:S(2)}) collective-permute-start(bf16[256,768]{1,0:T(8,128)(2,1)} %added.4.refs_3_), channel_id=1, source_target_pairs={{0,16},{2,18},{4,20},{6,22},{8,24},{10,26},{12,28},{14,30},{16,0},... | collective-permute-start | bytes 1179656 | tf_op jit(solution)/shard_map/ppermute | solution.py:465
  55.4 0.5 collective-permute-start.8
  56.0 6.0 %collective-permute-done.8.refs_1_ = f32[4,24,384]{2,1,0:T(8,128)S(1)} collective-permute-done((f32[4,24,384]{2,1,0:T(8,128)S(1)}, f32[4,24,384]{2,1,0:T(8,128)S(1)}, u32[]{:S(2)}, u32[]{:S(2)}) %collective-permute-start.8) | collective-permute-done | bytes 147488 | tf_op jit(solution)/shard_map/ppermute | solution.py:460
  62.0 0.8 %collective-permute-start.10 = (f32[2,24,384]{2,1,0:T(8,128)S(1)}, f32[2,24,384]{2,1,0:T(8,128)S(1)}, u32[]{:S(2)}, u32[]{:S(2)}) collective-permute-start(f32[2,24,384]{2,1,0:T(8,128)S(1)} %get-tuple-element.62), channel_id=1, source_target_pairs={{0,8},{2,10},{4,12},{6,14},{8,0},{10,2},{12,4},{14,6},{16,24},{18,... | collective-permute-start | bytes 221192 | tf_op jit(solution)/shard_map/ppermute | solution.py:460
  62.8 5.6 %collective-permute-done.10.refs_1_ = f32[2,24,384]{2,1,0:T(8,128)S(1)} collective-permute-done((f32[2,24,384]{2,1,0:T(8,128)S(1)}, f32[2,24,384]{2,1,0:T(8,128)S(1)}, u32[]{:S(2)}, u32[]{:S(2)}) %collective-permute-start.10) | collective-permute-done | bytes 73760 | tf_op jit(solution)/shard_map/ppermute | solution.py:460
  68.4 2.7 %collective-permute-start.11 = (f32[1,24,384]{2,1,0:T(8,128)S(1)}, f32[1,24,384]{2,1,0:T(8,128)S(1)}, u32[]{:S(2)}, u32[]{:S(2)}) collective-permute-start(f32[1,24,384]{2,1,0:T(8,128)S(1)} %get-tuple-element.64), channel_id=1, source_target_pairs={{0,16},{2,18},{4,20},{6,22},{8,24},{10,26},{12,28},{14,30},{16,0},... | collective-permute-start | bytes 110600 | tf_op jit(solution)/shard_map/ppermute | solution.py:460
  71.1 1.0 %constant_dynamic-slice_fusion.c_ref = bf16[256,768]{1,0:T(8,128)(2,1)S(1)} fusion(bf16[4096,768]{1,0:T(8,128)(2,1)} %param.7, s32[]{:T(128)S(6)} %select_n.4), kind=kLoop, calls=%fused_computation | loop fusion | bytes 786436 | tf_op jit(solution)/shard_map/dynamic_slice | solution.py:527
  72.1 0.8 %dynamic_slice.7 = f32[256]{0:T(256)S(1)} dynamic-slice(f32[4096]{0:T(1024)} %param.8, s32[]{:T(128)S(6)} %select_n.4), dynamic_slice_sizes={256} | dynamic-slice | bytes 2052 | tf_op jit(solution)/shard_map/dynamic_slice | solution.py:528
  72.9 0.0 collective-permute-done.12.refs_1_
  72.9 0.4 collective-permute-done.11.more_ref
  73.3 0.0 collective-permute-done.13.refs_2_
  73.3 0.0 collective-permute-done.14.refs_3_
  73.3 1.3 %update.1 = (f32[256,768]{1,0:T(8,128)}, f32[1,16,384]{2,1,0:T(8,128)}) custom-call(bf16[256,768]{1,0:T(8,128)(2,1)S(1)} %constant_dynamic-slice_fusion.c_ref, f32[1,256]{1,0:T(1,128)S(1)} %bitcast.7, f32[1,24,384]{2,1,0:T(8,128)S(1)} %get-tuple-element.63.small_ref, f32[1,24,384]{2,1,0:T(8,128)S(1)} %collective-permute-done.11.more_ref, ...), custom_call_target="tpu_custom_call" | custom-call | flops 1024 | bytes 1024 | tf_op jit(solution)/shard_map/update/pallas_call | solution.py:593
  (5 shorter events, 0.1 us)
Async XLA Ops:
  0.6 7.4 %collective-permute-start = (bf16[1024,768]{1,0:T(8,128)(2,1)}, bf16[1024,768]{1,0:T(8,128)(2,1)S(1)}, u32[]{:S(2)}, u32[]{:S(2)}) collective-permute-start(bf16[1024,768]{1,0:T(8,128)(2,1)} %v_ref.1), channel_id=1, source_target_pairs={{0,2},{2,0},{4,6},{6,4},{8,10},{10,8},{12,14},{14,12},{16,18},{18,... | collective-permute-start | bytes 4718600 | tf_op jit(solution)/shard_map/ppermute | solution.py:460
  8.1 4.4 %copy-start.2 = (s32[1024]{0:T(1024)S(1)}, s32[1024]{0:T(1024)}, u32[]{:S(2)}) copy-start(s32[1024]{0:T(1024)} %param.9) | copy-start | bytes 12292
  8.1 9.0 %copy-start = (bf16[768,768]{1,0:T(8,128)(2,1)S(1)}, bf16[768,768]{1,0:T(8,128)(2,1)}, u32[]{:S(2)}) copy-start(bf16[768,768]{1,0:T(8,128)(2,1)} %rot_ref.1) | copy-start | bytes 3538948
  8.1 9.0 %copy-start.1 = (s32[8192]{0:T(1024)S(1)}, s32[8192]{0:T(1024)}, u32[]{:S(2)}) copy-start(s32[8192]{0:T(1024)} %param.10) | copy-start | bytes 98308
  12.3 1.7 %collective-permute-start.1 = (f32[4,1024]{1,0:T(4,128)S(1)}, f32[4,1024]{1,0:T(4,128)S(1)}, u32[]{:S(2)}, u32[]{:S(2)}) collective-permute-start(f32[4,1024]{1,0:T(4,128)S(1)} %get-tuple-element.38._.a_ref), channel_id=1, source_target_pairs={{0,2},{2,0},{4,6},{6,4},{8,10},{10,8},{12,14},{14,12},{16,18},{18,... | collective-permute-start | bytes 49160 | tf_op jit(solution)/shard_map/ppermute | solution.py:460
  14.0 10.1 %collective-permute-start.2 = (f32[4,1024]{1,0:T(4,128)S(1)}, f32[4,1024]{1,0:T(4,128)S(1)}, u32[]{:S(2)}, u32[]{:S(2)}) collective-permute-start(f32[4,1024]{1,0:T(4,128)S(1)} %merge.1._.near_ref), channel_id=1, source_target_pairs={{0,1},{1,0},{2,3},{3,2},{4,5},{5,4},{6,7},{7,6},{8,9},{9,8},{10,11... | collective-permute-start | bytes 49160 | tf_op jit(solution)/shard_map/ppermute | solution.py:460
  25.8 9.1 %collective-permute-start.4 = (bf16[256,768]{1,0:T(8,128)(2,1)}, bf16[256,768]{1,0:T(8,128)(2,1)S(1)}, u32[]{:S(2)}, u32[]{:S(2)}) collective-permute-start(bf16[256,768]{1,0:T(8,128)(2,1)} %get-tuple-element.49), channel_id=1, source_target_pairs={{0,4},{2,10},{4,0},{6,14},{8,12},{10,2},{12,8},{14,6},{16,20},{18,... | collective-permute-start | bytes 1179656 | tf_op jit(solution)/shard_map/ppermute | solution.py:465
  31.0 6.0 %collective-permute-start.3 = (bf16[8,16,768]{2,1,0:T(8,128)(2,1)S(1)}, bf16[8,16,768]{2,1,0:T(8,128)(2,1)S(1)}, u32[]{:S(2)}, u32[]{:S(2)}) collective-permute-start(bf16[8,16,768]{2,1,0:T(8,128)(2,1)S(1)} %get-tuple-element.47), channel_id=1, source_target_pairs={{0,2},{2,0},{4,6},{6,4},{8,10},{10,8},{12,14},{14,12},{16,18},{18,... | collective-permute-start | bytes 589832 | tf_op jit(solution)/shard_map/ppermute | solution.py:460
  33.9 10.5 %collective-permute-start.6 = (bf16[256,768]{1,0:T(8,128)(2,1)}, bf16[256,768]{1,0:T(8,128)(2,1)S(1)}, u32[]{:S(2)}, u32[]{:S(2)}) collective-permute-start(bf16[256,768]{1,0:T(8,128)(2,1)} %get-tuple-element.55), channel_id=1, source_target_pairs={{0,4},{2,10},{4,0},{6,14},{8,12},{10,2},{12,8},{14,6},{16,20},{18,... | collective-permute-start | bytes 1179656 | tf_op jit(solution)/shard_map/ppermute | solution.py:465
  35.8 11.4 %collective-permute-start.7 = (bf16[256,768]{1,0:T(8,128)(2,1)}, bf16[256,768]{1,0:T(8,128)(2,1)S(1)}, u32[]{:S(2)}, u32[]{:S(2)}) collective-permute-start(bf16[256,768]{1,0:T(8,128)(2,1)} %added.3._), channel_id=1, source_target_pairs={{0,8},{2,6},{4,12},{6,2},{8,0},{10,14},{12,4},{14,10},{16,24},{18,... | collective-permute-start | bytes 1179656 | tf_op jit(solution)/shard_map/ppermute | solution.py:465
  41.2 9.1 %collective-permute-start.9 = (bf16[256,768]{1,0:T(8,128)(2,1)}, bf16[256,768]{1,0:T(8,128)(2,1)S(1)}, u32[]{:S(2)}, u32[]{:S(2)}) collective-permute-start(bf16[256,768]{1,0:T(8,128)(2,1)} %get-tuple-element.60), channel_id=1, source_target_pairs={{0,4},{2,10},{4,0},{6,14},{8,12},{10,2},{12,8},{14,6},{16,20},{18,... | collective-permute-start | bytes 1179656 | tf_op jit(solution)/shard_map/ppermute | solution.py:465
  42.8 5.7 %collective-permute-start.5 = (f32[8,16,384]{2,1,0:T(8,128)S(1)}, f32[8,16,384]{2,1,0:T(8,128)S(1)}, u32[]{:S(2)}, u32[]{:S(2)}) collective-permute-start(f32[8,16,384]{2,1,0:T(8,128)S(1)} %get-tuple-element.52), channel_id=1, source_target_pairs={{0,1},{1,0},{2,3},{3,2},{4,5},{5,4},{6,7},{7,6},{8,9},{9,8},{10,11... | collective-permute-start | bytes 589832 | tf_op jit(solution)/shard_map/ppermute | solution.py:460
  43.3 29.5 %collective-permute-start.12 = (bf16[256,768]{1,0:T(8,128)(2,1)}, bf16[256,768]{1,0:T(8,128)(2,1)S(1)}, u32[]{:S(2)}, u32[]{:S(2)}) collective-permute-start(bf16[256,768]{1,0:T(8,128)(2,1)} %get-tuple-element.65), channel_id=1, source_target_pairs={{0,4},{2,10},{4,0},{6,14},{8,12},{10,2},{12,8},{14,6},{16,20},{18,... | collective-permute-start | bytes 1179656 | tf_op jit(solution)/shard_map/ppermute | solution.py:465
  51.2 22.1 %collective-permute-start.13 = (bf16[256,768]{1,0:T(8,128)(2,1)}, bf16[256,768]{1,0:T(8,128)(2,1)S(1)}, u32[]{:S(2)}, u32[]{:S(2)}) collective-permute-start(bf16[256,768]{1,0:T(8,128)(2,1)} %added.5.refs_2_), channel_id=1, source_target_pairs={{0,8},{2,6},{4,12},{6,2},{8,0},{10,14},{12,4},{14,10},{16,24},{18,... | collective-permute-start | bytes 1179656 | tf_op jit(solution)/shard_map/ppermute | solution.py:465
  52.9 20.4 %collective-permute-start.14 = (bf16[256,768]{1,0:T(8,128)(2,1)}, bf16[256,768]{1,0:T(8,128)(2,1)S(1)}, u32[]{:S(2)}, u32[]{:S(2)}) collective-permute-start(bf16[256,768]{1,0:T(8,128)(2,1)} %added.4.refs_3_), channel_id=1, source_target_pairs={{0,16},{2,18},{4,20},{6,22},{8,24},{10,26},{12,28},{14,30},{16,0},... | collective-permute-start | bytes 1179656 | tf_op jit(solution)/shard_map/ppermute | solution.py:465
  55.4 6.5 %collective-permute-start.8 = (f32[4,24,384]{2,1,0:T(8,128)S(1)}, f32[4,24,384]{2,1,0:T(8,128)S(1)}, u32[]{:S(2)}, u32[]{:S(2)}) collective-permute-start(f32[4,24,384]{2,1,0:T(8,128)S(1)} %get-tuple-element.58), channel_id=1, source_target_pairs={{0,4},{2,6},{4,0},{6,2},{8,12},{10,14},{12,8},{14,10},{16,20},{18,... | collective-permute-start | bytes 442376 | tf_op jit(solution)/shard_map/ppermute | solution.py:460
  62.0 6.4 %collective-permute-start.10 = (f32[2,24,384]{2,1,0:T(8,128)S(1)}, f32[2,24,384]{2,1,0:T(8,128)S(1)}, u32[]{:S(2)}, u32[]{:S(2)}) collective-permute-start(f32[2,24,384]{2,1,0:T(8,128)S(1)} %get-tuple-element.62), channel_id=1, source_target_pairs={{0,8},{2,10},{4,12},{6,14},{8,0},{10,2},{12,4},{14,6},{16,24},{18,... | collective-permute-start | bytes 221192 | tf_op jit(solution)/shard_map/ppermute | solution.py:460
  68.4 4.9 %collective-permute-start.11 = (f32[1,24,384]{2,1,0:T(8,128)S(1)}, f32[1,24,384]{2,1,0:T(8,128)S(1)}, u32[]{:S(2)}, u32[]{:S(2)}) collective-permute-start(f32[1,24,384]{2,1,0:T(8,128)S(1)} %get-tuple-element.64), channel_id=1, source_target_pairs={{0,16},{2,18},{4,20},{6,22},{8,24},{10,26},{12,28},{14,30},{16,0},... | collective-permute-start | bytes 110600 | tf_op jit(solution)/shard_map/ppermute | solution.py:460

commit v3 on v2

--- a/solution.py
+++ b/solution.py
@@ -10,6 +10,8 @@
 
 M = 48
 CHUNK = 256
+SPARE = 16
+EARLY = 3
 F32 = jnp.float32
 BF16 = jnp.bfloat16
 HBM = pl.BlockSpec(memory_space=pltpu.HBM)
@@ -75,10 +77,10 @@
     chunks = range(0, c_ref.shape[0], CHUNK)
     peak = None
     ahead = product(0)
-    if ready is not None:
-        ready()
     for place, k in enumerate(chunks):
         now = ahead
+        if ready is not None and place + 1 == EARLY:
+            ready()
         if place + 1 < len(chunks):
             ahead = product(chunks[place + 1])
         c = c_ref[k : k + CHUNK].astype(F32)
@@ -102,13 +104,15 @@
         for k, p in enumerate(places)
     ]
     whole = pltpu.make_async_copy(v_ref, vh_ref, v_sem)
-    early = CHUNK // rows
+    early = EARLY * CHUNK // rows
     whole.start()
-    for copy in copies:
+    for copy in copies[:early]:
         copy.start()
     for copy in copies[:early]:
         copy.wait()
     whole.wait()
+    for copy in copies[early:]:
+        copy.start()
 
     def rest():
         for copy in copies[early:]:
@@ -345,9 +349,8 @@
     )(in_vmem(picked), in_vmem(ids), in_vmem(c_half), in_hbm(c_blocks), owner, rotation, token)
 
 
-def moment_kernel(r_ref, own_ref, _, __, ___, keep_ref, send_ref, all_ref, *, sub, order):
+def moment_kernel(r_ref, own_ref, _, __, ___, mine_ref, theirs_ref, all_ref, *, sub, order, split):
     rows, width = r_ref.shape
-    half = len(order)
     tile = 256 if width % 256 == 0 else width
     own = own_ref[...].T[0:1, :]
     diagonal = (lax.broadcasted_iota(jnp.int32, (tile, tile), 0) // sub) == (
@@ -362,16 +365,23 @@
         for place, hit in enumerate(hits):
             gram = jnp.where(diagonal, dot(turned * hit, r, 1, 0), 0.0)
             all_ref[place, :, t : t + tile] = jnp.sum(gram.reshape(tile // sub, sub, tile), axis=0)
-    keep_ref[...] = all_ref[:half]
-    send_ref[...] = all_ref[half:].astype(send_ref.dtype)
-
-
-def owner_moments(order, rotated, own, token, s1, s2, sub):
+    if split:
+        size = mine_ref.shape[2]
+        cent_pos = lax.axis_index("cent")
+        for ref, side in ((mine_ref, cent_pos), (theirs_ref, 1 - cent_pos)):
+            part = all_ref[:, :, pl.ds(pl.multiple_of(side * size, 128), size)]
+            ref[...] = part.astype(ref.dtype)
+    else:
+        mine_ref[...] = all_ref[...]
+        theirs_ref[...] = jnp.zeros_like(theirs_ref)
+
+
+def owner_moments(order, rotated, own, token, s1, s2, sub, split):
     rows, width = rotated.shape
     half = len(order)
-    shape = (half, sub, width)
-    return pl.pallas_call(
-        functools.partial(moment_kernel, sub=sub, order=order),
+    shape = (2 * half, sub, width // 2 if split else width)
+    return pl.pallas_call(
+        functools.partial(moment_kernel, sub=sub, order=order, split=split),
         in_specs=[VMEM, VMEM, ANY, VMEM, VMEM],
         out_specs=[VMEM] * 2,
         out_shape=[jax.ShapeDtypeStruct(shape, F32), jax.ShapeDtypeStruct(shape, BF16)],
@@ -382,25 +392,22 @@
     )(in_vmem(rotated), in_vmem(own), token, in_vmem(s1), in_vmem(s2))
 
 
-def side_kernel(a_ref, b_ref, _, mine_ref, theirs_ref, all_ref):
-    all_ref[...] = a_ref[...] + b_ref[...].astype(F32)
-    size = mine_ref.shape[2]
-    cent_pos = lax.axis_index("cent")
-    for ref, side in ((mine_ref, cent_pos), (theirs_ref, 1 - cent_pos)):
-        ref[...] = all_ref[:, :, pl.ds(pl.multiple_of(side * size, 128), size)]
-
-
-def sides(a, b, token):
+def core_kernel(a_ref, b_ref, _, keep_ref, send_ref):
+    half = keep_ref.shape[0]
+    keep_ref[...] = a_ref[:half] + b_ref[:half].astype(F32)
+    send_ref[...] = a_ref[half:] + b_ref[half:].astype(F32)
+
+
+def by_core(a, b, token):
     n, sub, width = a.shape
     return pl.pallas_call(
-        side_kernel,
+        core_kernel,
         in_specs=[VMEM, VMEM, ANY],
         out_specs=[VMEM] * 2,
-        out_shape=[jax.ShapeDtypeStruct((n, sub, width // 2), F32)] * 2,
-        scratch_shapes=[pltpu.VMEM(a.shape, F32)],
+        out_shape=[jax.ShapeDtypeStruct((n // 2, sub, width), F32)] * 2,
         compiler_params=params(6),
         cost_estimate=cost(0),
-        name="sides",
+        name="by_core",
     )(a, b, token)
 
 
@@ -433,25 +440,26 @@
     )(*parts, mass, token)
 
 
-def halves_kernel(*refs, n):
+def split_kernel(*refs, n):
+    outs = refs[n + 1 :]
     total = refs[0][...]
     for part in refs[1:n]:
         total = total + part[...]
-    size = total.shape[0] // 2
-    refs[n + 1][...] = total[:size]
-    refs[n + 2][...] = total[size:]
-
-
-def halves(parts, token):
+    size = outs[0].shape[0]
+    for k, ref in enumerate(outs):
+        ref[...] = total[k * size : (k + 1) * size]
+
+
+def split_sum(parts, count, token):
     n, rows, width = parts[0].shape
     return pl.pallas_call(
-        functools.partial(halves_kernel, n=len(parts)),
+        functools.partial(split_kernel, n=len(parts)),
         in_specs=[VMEM] * len(parts) + [ANY],
-        out_specs=[VMEM] * 2,
-        out_shape=[jax.ShapeDtypeStruct((n // 2, rows, width), F32)] * 2,
+        out_specs=[VMEM] * count,
+        out_shape=[jax.ShapeDtypeStruct((n // count, rows, width), F32)] * count,
         compiler_params=params(4),
         cost_estimate=cost(0),
-        name="halves",
+        name="split_sum",
     )(*parts, token)
 
 
@@ -475,14 +483,16 @@
     total = parts[0][starts[0] : starts[0] + rows].astype(F32)
     for part, start in zip(parts[1:], starts[1:]):
         total = total + part[start : start + rows].astype(F32)
-    stage[...] = total.astype(stage.dtype)
+    stage[:rows] = total.astype(stage.dtype)
+    if stage.shape[0] > rows:
+        stage[rows:] = jnp.zeros((stage.shape[0] - rows, stage.shape[1]), stage.dtype)
     copy = pltpu.make_async_copy(stage, o_ref, sem)
     copy.start()
     copy.wait()
 
 
-def added(parts, starts, rows, *tokens):
-    shape = (rows, parts[0].shape[1])
+def added(parts, starts, rows, *tokens, spare=0):
+    shape = (rows + spare, parts[0].shape[1])
     return pl.pallas_call(
         functools.partial(add_kernel, starts=starts, rows=rows),
         in_specs=[VMEM] * len(parts) + [ANY] * len(tokens),
@@ -495,11 +505,14 @@
     )(*parts, *tokens)
 
 
-def update_kernel(c_ref, prior_ref, small_ref, more_ref, *refs, count, parts):
+def update_kernel(c_ref, prior_ref, *refs, count, smalls, parts):
     o_ref, moment_ref = refs[-2:]
     rows = o_ref.shape[0]
     sub = moment_ref.shape[1]
-    small = small_ref[0] + more_ref[0]
+    small = refs[0][0]
+    for ref in refs[1:smalls]:
+        small = small + ref[0]
+    refs = refs[smalls:]
     moment_ref[0] = small[:sub] * (1.0 / count)
     prior = prior_ref[...]
     inverse = 1.0 / (prior + small[sub : sub + 1, :rows])
@@ -508,7 +521,7 @@
     for k, n in enumerate(parts):
         total = refs[0][...].astype(F32)
         for ref in refs[1:n]:
-            total = total + ref[...].astype(F32)
+            total = total + ref[: total.shape[0]].astype(F32)
         refs = refs[n:]
         here = slice(start, start + total.shape[0])
         start += total.shape[0]
@@ -556,43 +569,44 @@
     came3 = exchange(got3, 0)
 
     order = [reverse_bits(k, levels) for k in range(1 << levels)]
-    keep, sent = owner_moments(order, rotated, own, mass, s1, s2, width // M)
-    sent = flip(sent, "dp", 1)
-    got2, kept3, kept2, mass = sums(mass, ("send2", "keep3", "keep2"), keep)
+    split = cent_count == 2
+    mine, theirs = owner_moments(order, rotated, own, mass, s1, s2, width // M, split)
+    theirs = flip(theirs, "cent", 1) if split else theirs
+    got2, kept3, kept2, mass = sums(mass, ("send2", "keep3", "keep2"), mine)
     came2 = exchange(got2, 0)
     n = kept3.shape[0]
     next3 = added([kept3, came3], [0, 0], n, mass)
     over3 = exchange(next3, 1)
-    if cent_count == 2:
-        keep, sent = sides(keep, sent, in_hbm(next3))
-        moments = [keep, flip(sent, "cent", 1)]
-    else:
-        moments = [lax.psum_scatter(joined(keep, sent), "cent", scatter_dimension=2, tiled=True)]
+    if not split:
+        mine = lax.psum_scatter(mine, "cent", scatter_dimension=2, tiled=True)
+        theirs = jnp.zeros_like(mine)
+    keep, sent = by_core(mine, theirs, in_hbm(next3))
+    moments = [keep, flip(sent, "dp", 1)]
     got1, got0, kept1, kept0, mass = sums(mass, ("send1", "send0", "keep1", "keep0"), keep)
     came1, came0 = exchange(got1, 0), exchange(got0, 0)
-    next2 = added([kept2, came2, over3], [0, 0, 0], n, kept0)
+
+    keep, sent = packed(moments, mass, kept0)
+    small = [keep, flip(sent, "dp", 2)]
+    next2 = added([kept2, came2, over3], [0, 0, 0], n, keep, spare=SPARE)
     over2 = exchange(next2, 2)
-
-    keep, sent = packed(moments, mass, in_hbm(next2))
-    small = [keep, flip(sent, "dp", 2)]
+    keep, over_b, over_a, over_ab = split_sum(small, 4, in_hbm(next2))
+    small = [keep, flip(over_a, "dp", 4), flip(over_b, "dp", 8), flip(over_ab, "dp", 12)]
     next1 = added([kept1, came1], [0, 0], n, keep)
     over1 = exchange(next1, 1)
-    token = in_hbm(next1)
-    for level in range(1, levels):
-        keep, sent = halves(small, token)
+    for level in range(3, levels):
+        keep, sent = split_sum(small, 2, small[0])
         small = [keep, flip(sent, "dp", 2 << level)]
-        token = keep
     parts = [[kept0, came0, over1, over2]]
     level = 3
     while level < levels:
-        total = jnp.concatenate([sum(p.astype(F32) for p in part) for part in parts])
+        total = sum(p[: parts[0][0].shape[0]].astype(F32) for p in parts[0])
         n = total.shape[0] // 2
         parts = [[total[:n], exchange(total[n:].astype(BF16), level)]]
         level += 1
     sub, near_half = width // M, width // cent_count
     updated, moments = pl.pallas_call(
-        functools.partial(update_kernel, count=row_count, parts=tuple(len(part) for part in parts)),
-        in_specs=[VMEM] * (4 + sum(len(part) for part in parts)),
+        functools.partial(update_kernel, count=row_count, smalls=len(small), parts=tuple(len(part) for part in parts)),
+        in_specs=[VMEM] * (2 + len(small) + sum(len(part) for part in parts)),
         out_specs=[VMEM] * 2,
         out_shape=[
             jax.ShapeDtypeStruct((block, width), F32),

time: 74.8 us -> 72 us (0.963)
  waiting for transfers between devices: 17.6 us -> 12.1 us
  starting transfers between devices: 18.4 us -> 21.8 us
    ppermute x7, waiting for transfers between devices: 5.23 us -> 1.7 us  [exchange(): return lax.ppermute(array, 'dp', [(i, i ^ far[i % 2]) for i in range(size)])]
    ppermute x8 -> x9, starting transfers between devices: 8.27 us -> 10.5 us  [flip(): return lax.ppermute(array, axis, [(i, i ^ mask) for i in range(size)])]
    ppermute x8 -> x9, waiting for transfers between devices: 12.4 us -> 10.4 us  [flip(): return lax.ppermute(array, axis, [(i, i ^ mask) for i in range(size)])]
    ppermute x7, starting transfers between devices: 10.1 us -> 11.3 us  [exchange(): return lax.ppermute(array, 'dp', [(i, i ^ far[i % 2]) for i in range(size)])]
    pallas_call x5 -> x4, Pallas kernels: 4.98 us -> 4.92 us  [the longest x1 3.58 us: owner_moments(): pl.pallas_call(functools.partial(moment_kernel, sub=sub, order=order, spl...]
  transfers between devices with their start and end apart: 15 -> 16, of which waited for: 7 -> 4; matrix products, arithmetic and copies ran while one was open for 2% -> 2% of each run, Pallas kernels for 39% -> 39%
where the time goes in v3:
time: 72 us; the launch traced here: 71.8 us
  Pallas kernels  35.3 us (49%)
  starting transfers between devices  21.8 us (30%)
  waiting for transfers between devices  12.1 us (17%)
  local copies, waits for them, and re-layouts  1.81 us (3%)
  between operations  0.81 us (1%)
    ppermute x7, starting transfers between devices, exchange(): return lax.ppermute(array, 'dp', [(i, i ^ far[i % 2]) for i in range(size)])  11.3 us
    ppermute x9, starting transfers between devices, flip(): return lax.ppermute(array, axis, [(i, i ^ mask) for i in range(size)])  10.5 us
    ppermute x9, waiting for transfers between devices, flip(): return lax.ppermute(array, axis, [(i, i ^ mask) for i in range(size)])  10.4 us
    pallas_call x3, Pallas kernels, sums_of(): pl.pallas_call(functools.partial(sums_kernel, which=which, sends=sends, r...  8.73 us
    pallas_call x1, Pallas kernels, rotated_residuals(): pl.pallas_call(functools.partial(residual_kernel, places=places), in_spec...  7.01 us
    pallas_call x1, Pallas kernels, first_scores(): pl.pallas_call(functools.partial(first_scores_kernel, places=places, scal...  6.27 us
    pallas_call x1, Pallas kernels, second_scores(): pl.pallas_call(functools.partial(second_scores_kernel, scale=scale), in_s...  4.21 us
    pallas_call x1, Pallas kernels, owner_moments(): pl.pallas_call(functools.partial(moment_kernel, sub=sub, order=order, spl...  3.58 us
  transfers between devices with their start and end apart: 16, of which 4 were waited for; matrix products, arithmetic and copies ran while one was open for 2% of the time, Pallas kernels for 39%

profile of v3, /device:TPU:0, one launch (start us, length us, event | category | flops | bytes accessed | tf_op | source)
XLA Modules:
  0.0 71.8 jit_solution(18299856938465936573)
XLA Ops:
  0.6 0.5 collective-permute-start
  1.1 6.3 %first_scores.1 = (f32[2048,1024]{1,0:T(8,128)S(1)}, f32[2,1024]{1,0:T(2,128)S(1)}, bf16[2048,768]{1,0:T(8,128)(2,1)S(1)}, bf16[1024,768]{1,0:T(8,128)(2,1)S(1)}) custom-call(bf16[1024,768]{1,0:T(8,128)(2,1)} %v_ref.1, bf16[16,256,768]{2,1,0:T(8,128)(2,1)} %bitcast.8), custom_call_target="tpu_custom_call" | custom-call | flops 1024 | bytes 1024 | tf_op jit(solution)/shard_map/first_scores/pallas_call | solution.py:129
  7.4 0.0 copy-start.2
  7.4 0.0 collective-permute-done.v_ref.v2_ref
  7.4 0.0 copy-start
  7.5 0.0 copy-start.1
  7.5 4.2 %second_scores.1 = (f32[2048,1024]{1,0:T(8,128)S(1)}, f32[4,1024]{1,0:T(4,128)S(1)}) custom-call(bf16[1024,768]{1,0:T(8,128)(2,1)S(1)} %collective-permute-done.v_ref.v2_ref, bf16[2048,768]{1,0:T(8,128)(2,1)S(1)} %get-tuple-element.36.ch_ref.near_ref, f32[2,1024]{1,0:T(2,128)S(1)} %get-tuple-element.37.st_ref), custom_call_target="tpu_custom_call" | custom-call | flops 1024 | bytes 1024 | tf_op jit(solution)/shard_map/second_scores/pallas_call | solution.py:156
  11.7 0.1 collective-permute-start.1
  11.8 0.0 copy-done.2
  11.8 1.6 %picked.1 = (bf16[512,768]{1,0:T(8,128)(2,1)S(1)}, s32[512,128]{1,0:T(8,128)S(1)}) custom-call(s32[1,1024]{1,0:T(1,128)S(1)} %bitcast.6, bf16[1024,768]{1,0:T(8,128)(2,1)S(1)} %get-tuple-element.35.v_ref.v1_ref, f32[4,1024]{1,0:T(4,128)S(1)} %get-tuple-element.38._.a_ref), custom_call_target="tpu_custom_call" | custom-call | flops 1024 | bytes 1024 | tf_op jit(solution)/shard_map/picked/pallas_call | solution.py:280
  13.3 0.0 collective-permute-done.1.b_ref
  13.4 3.0 %collective-permute-start.2 = (f32[4,1024]{1,0:T(4,128)S(1)}, f32[4,1024]{1,0:T(4,128)S(1)}, u32[]{:S(2)}, u32[]{:S(2)}) collective-permute-start(f32[4,1024]{1,0:T(4,128)S(1)} %merge.1._.near_ref), channel_id=1, source_target_pairs={{0,1},{1,0},{2,3},{3,2},{4,5},{5,4},{6,7},{7,6},{8,9},{9,8},{10,11... | collective-permute-start | bytes 49160 | tf_op jit(solution)/shard_map/ppermute | solution.py:468
  16.4 0.0 copy-done
  16.4 0.0 copy-done.1
  16.4 7.0 %residuals.1 = (bf16[512,768]{1,0:T(8,128)(2,1)S(1)}, f32[512,128]{1,0:T(8,128)S(1)}) custom-call(bf16[512,768]{1,0:T(8,128)(2,1)S(1)} %get-tuple-element.39.picked_ref, s32[512,128]{1,0:T(8,128)S(1)} %get-tuple-element.40._.ids_ref, bf16[2048,768]{1,0:T(8,128)(2,1)S(1)} %get-tuple-element.36.ch_ref.near_ref, bf16[16,256,768]{2,1,0:T(8,128)(2,1)} %bitcast.9, ...), custom_call_target="tpu_custom_call" | custom-call | flops 1024 | bytes 1024 | tf_op jit(solution)/shard_map/residuals/pallas_call | solution.py:337
  23.4 0.0 collective-permute-done.2.far_ref
  23.5 1.7 %sums.3 = (bf16[256,768]{1,0:T(8,128)(2,1)}, f32[8,256]{1,0:T(8,128)S(1)}) custom-call(f32[2048,1024]{1,0:T(8,128)S(1)} %get-tuple-element.43.s1_ref.__, f32[2048,1024]{1,0:T(8,128)S(1)} %get-tuple-element.44.s2_ref.___, f32[4,1024]{1,0:T(4,128)S(1)} %merge.1._.near_ref, f32[4,1024]{1,0:T(4,128)S(1)} %collective-permute-done.2.far_ref, ...), custom_call_target="tpu_custom_call" | custom-call | flops 1024 | bytes 1024 | tf_op jit(solution)/shard_map/sums/pallas_call | solution.py:246
  25.2 1.6 %collective-permute-start.4 = (bf16[256,768]{1,0:T(8,128)(2,1)}, bf16[256,768]{1,0:T(8,128)(2,1)S(1)}, u32[]{:S(2)}, u32[]{:S(2)}) collective-permute-start(bf16[256,768]{1,0:T(8,128)(2,1)} %get-tuple-element.49), channel_id=1, source_target_pairs={{0,4},{2,10},{4,0},{6,14},{8,12},{10,2},{12,8},{14,6},{16,20},{18,... | collective-permute-start | bytes 1179656 | tf_op jit(solution)/shard_map/ppermute | solution.py:473
  26.8 3.6 %moments.1 = (f32[16,16,384]{2,1,0:T(8,128)S(1)}, bf16[16,16,384]{2,1,0:T(8,128)(2,1)S(1)}) custom-call(bf16[512,768]{1,0:T(8,128)(2,1)S(1)} %get-tuple-element.41.r_ref, f32[512,128]{1,0:T(8,128)S(1)} %get-tuple-element.42._.own_ref, f32[8,256]{1,0:T(8,128)S(1)} %get-tuple-element.45._.old_ref, f32[2048,1024]{1,0:T(8,128)S(1)} %get-tuple-element.43.s1_ref.__, ...), custom_call_target="tpu_custom_call" | custom-call | flops 1024 | bytes 1024 | tf_op jit(solution)/shard_map/moments/pallas_call | solution.py:383
  30.3 0.6 collective-permute-start.3
  30.9 2.8 %sums.4 = (bf16[256,768]{1,0:T(8,128)(2,1)}, f32[256,768]{1,0:T(8,128)S(1)}, f32[256,768]{1,0:T(8,128)S(1)}, f32[8,256]{1,0:T(8,128)S(1)}) custom-call(f32[2048,1024]{1,0:T(8,128)S(1)} %get-tuple-element.43.s1_ref.__, f32[2048,1024]{1,0:T(8,128)S(1)} %get-tuple-element.44.s2_ref.___, f32[4,1024]{1,0:T(4,128)S(1)} %merge.1._.near_ref, ...), custom_call_target="tpu_custom_call" | custom-call | flops 1024 | bytes 1024 | tf_op jit(solution)/shard_map/sums/pallas_call | solution.py:246
  33.7 0.1 collective-permute-start.7
  33.9 0.0 collective-permute-done.4.refs_1_
  33.9 0.8 %added.3._ = bf16[256,768]{1,0:T(8,128)(2,1)} custom-call(f32[256,768]{1,0:T(8,128)S(1)} %get-tuple-element.48.refs_0_, bf16[256,768]{1,0:T(8,128)(2,1)S(1)} %collective-permute-done.4.refs_1_, f32[8,256]{1,0:T(8,128)S(1)} %get-tuple-element.50.refs_2_.old_ref), custom_call_target="tpu_custom_call" | custom-call | flops 1024 | bytes 1024 | tf_op jit(solution)/shard_map/added/pallas_call | solution.py:496
  34.7 2.1 %collective-permute-start.8 = (bf16[256,768]{1,0:T(8,128)(2,1)}, bf16[256,768]{1,0:T(8,128)(2,1)S(1)}, u32[]{:S(2)}, u32[]{:S(2)}) collective-permute-start(bf16[256,768]{1,0:T(8,128)(2,1)} %added.3._), channel_id=1, source_target_pairs={{0,8},{2,6},{4,12},{6,2},{8,0},{10,14},{12,4},{14,10},{16,24},{18,... | collective-permute-start | bytes 1179656 | tf_op jit(solution)/shard_map/ppermute | solution.py:473
  36.8 0.0 collective-permute-done.3.b_ref
  36.9 4.2 %sums.5 = (bf16[256,768]{1,0:T(8,128)(2,1)}, bf16[256,768]{1,0:T(8,128)(2,1)}, f32[256,768]{1,0:T(8,128)S(1)}, f32[256,768]{1,0:T(8,128)S(1)}, f32[8,256]{1,0:T(8,128)S(1)}) custom-call(f32[2048,1024]{1,0:T(8,128)S(1)} %get-tuple-element.43.s1_ref.__, f32[2048,1024]{1,0:T(8,128)S(1)} %get-tuple-element.44.s2_ref.___, f32[4,1024]{1,0:T(4,128)S(1)} %merge.1._.near_ref, ...), custom_call_target="tpu_custom_call" | custom-call | flops 1024 | bytes 1024 | tf_op jit(solution)/shard_map/sums/pallas_call | solution.py:246
  41.1 1.5 %collective-permute-start.13 = (bf16[256,768]{1,0:T(8,128)(2,1)}, bf16[256,768]{1,0:T(8,128)(2,1)S(1)}, u32[]{:S(2)}, u32[]{:S(2)}) collective-permute-start(bf16[256,768]{1,0:T(8,128)(2,1)} %get-tuple-element.65), channel_id=1, source_target_pairs={{0,4},{2,10},{4,0},{6,14},{8,12},{10,2},{12,8},{14,6},{16,20},{18,... | collective-permute-start | bytes 1179656 | tf_op jit(solution)/shard_map/ppermute | solution.py:473
  42.6 0.0 collective-permute-start.5
  42.6 1.4 %collective-permute-done.5.refs_1_ = f32[8,16,384]{2,1,0:T(8,128)S(1)} collective-permute-done((f32[8,16,384]{2,1,0:T(8,128)S(1)}, f32[8,16,384]{2,1,0:T(8,128)S(1)}, u32[]{:S(2)}, u32[]{:S(2)}) %collective-permute-start.5) | collective-permute-done | bytes 196640 | tf_op jit(solution)/shard_map/ppermute | solution.py:468
  44.1 0.6 collective-permute-start.6
  44.7 1.5 %collective-permute-start.12 = (bf16[256,768]{1,0:T(8,128)(2,1)}, bf16[256,768]{1,0:T(8,128)(2,1)S(1)}, u32[]{:S(2)}, u32[]{:S(2)}) collective-permute-start(bf16[256,768]{1,0:T(8,128)(2,1)} %get-tuple-element.63), channel_id=1, source_target_pairs={{0,4},{2,10},{4,0},{6,14},{8,12},{10,2},{12,8},{14,6},{16,20},{18,... | collective-permute-start | bytes 1179656 | tf_op jit(solution)/shard_map/ppermute | solution.py:473
  46.2 0.0 collective-permute-done.7.refs_1_
  46.2 0.0 collective-permute-done.8.refs_2_
  46.2 0.9 %added.4.refs_2_ = bf16[272,768]{1,0:T(8,128)(2,1)} custom-call(f32[256,768]{1,0:T(8,128)S(1)} %get-tuple-element.57.refs_0_, bf16[256,768]{1,0:T(8,128)(2,1)S(1)} %collective-permute-done.7.refs_1_, bf16[256,768]{1,0:T(8,128)(2,1)S(1)} %collective-permute-done.8.refs_2_, f32[4,24,384]{2,1,0:T(8,128)S(1)} %get-tuple-element.55.refs_3_.refs_0_), custom_call_target="tpu_custom_call" | custom-call | flops 1024 | bytes 1024 | tf_op jit(solution)/shard_map/added/pallas_call | solution.py:496
  47.1 2.7 %collective-permute-start.15 = (bf16[272,768]{1,0:T(8,128)(2,1)}, bf16[272,768]{1,0:T(8,128)(2,1)S(1)}, u32[]{:S(2)}, u32[]{:S(2)}) collective-permute-start(bf16[272,768]{1,0:T(8,128)(2,1)} %added.4.refs_2_), channel_id=1, source_target_pairs={{0,16},{2,18},{4,20},{6,22},{8,24},{10,26},{12,28},{14,30},{16,0},... | collective-permute-start | bytes 1253384 | tf_op jit(solution)/shard_map/ppermute | solution.py:473
  49.7 2.9 %collective-permute-done.6.refs_1_ = f32[4,24,384]{2,1,0:T(8,128)S(1)} collective-permute-done((f32[4,24,384]{2,1,0:T(8,128)S(1)}, f32[4,24,384]{2,1,0:T(8,128)S(1)}, u32[]{:S(2)}, u32[]{:S(2)}) %collective-permute-start.6) | collective-permute-done | bytes 147488 | tf_op jit(solution)/shard_map/ppermute | solution.py:468
  52.6 0.0 collective-permute-done.13.refs_1_
  52.7 0.8 %added.5 = bf16[256,768]{1,0:T(8,128)(2,1)} custom-call(f32[256,768]{1,0:T(8,128)S(1)} %get-tuple-element.64.refs_0_, bf16[256,768]{1,0:T(8,128)(2,1)S(1)} %collective-permute-done.13.refs_1_, f32[1,24,384]{2,1,0:T(8,128)S(1)} %get-tuple-element.59.refs_2_.refs_0_), custom_call_target="tpu_custom_call" | custom-call | flops 1024 | bytes 1024 | tf_op jit(solution)/shard_map/added/pallas_call | solution.py:496
  53.5 1.8 %collective-permute-start.14 = (bf16[256,768]{1,0:T(8,128)(2,1)}, bf16[256,768]{1,0:T(8,128)(2,1)S(1)}, u32[]{:S(2)}, u32[]{:S(2)}) collective-permute-start(bf16[256,768]{1,0:T(8,128)(2,1)} %added.5), channel_id=1, source_target_pairs={{0,8},{2,6},{4,12},{6,2},{8,0},{10,14},{12,4},{14,10},{16,24},{18,... | collective-permute-start | bytes 1179656 | tf_op jit(solution)/shard_map/ppermute | solution.py:473
  55.3 2.6 %collective-permute-start.10 = (f32[1,24,384]{2,1,0:T(8,128)S(1)}, f32[1,24,384]{2,1,0:T(8,128)S(1)}, u32[]{:S(2)}, u32[]{:S(2)}) collective-permute-start(f32[1,24,384]{2,1,0:T(8,128)S(1)} %get-tuple-element.61), channel_id=1, source_target_pairs={{0,16},{2,18},{4,20},{6,22},{8,24},{10,26},{12,28},{14,30},{16,0},... | collective-permute-start | bytes 110600 | tf_op jit(solution)/shard_map/ppermute | solution.py:468
  57.9 0.1 collective-permute-start.11
  58.0 1.7 %collective-permute-done.12.refs_5_ = bf16[256,768]{1,0:T(8,128)(2,1)S(1)} collective-permute-done((bf16[256,768]{1,0:T(8,128)(2,1)}, bf16[256,768]{1,0:T(8,128)(2,1)S(1)}, u32[]{:S(2)}, u32[]{:S(2)}) %collective-permute-start.12) | collective-permute-done | bytes 393248 | tf_op jit(solution)/shard_map/ppermute | solution.py:473
  59.6 3.0 %collective-permute-start.9 = (f32[1,24,384]{2,1,0:T(8,128)S(1)}, f32[1,24,384]{2,1,0:T(8,128)S(1)}, u32[]{:S(2)}, u32[]{:S(2)}) collective-permute-start(f32[1,24,384]{2,1,0:T(8,128)S(1)} %get-tuple-element.60), channel_id=1, source_target_pairs={{0,8},{2,10},{4,12},{6,14},{8,0},{10,2},{12,4},{14,6},{16,24},{18,... | collective-permute-start | bytes 110600 | tf_op jit(solution)/shard_map/ppermute | solution.py:468
  62.6 1.0 %constant_dynamic-slice_fusion.c_ref = bf16[256,768]{1,0:T(8,128)(2,1)S(1)} fusion(bf16[4096,768]{1,0:T(8,128)(2,1)} %param.7, s32[]{:T(128)S(6)} %select_n.4), kind=kLoop, calls=%fused_computation | loop fusion | bytes 786436 | tf_op jit(solution)/shard_map/dynamic_slice | solution.py:540
  63.6 0.8 %dynamic_slice.7 = f32[256]{0:T(256)S(1)} dynamic-slice(f32[4096]{0:T(1024)} %param.8, s32[]{:T(128)S(6)} %select_n.4), dynamic_slice_sizes={256} | dynamic-slice | bytes 2052 | tf_op jit(solution)/shard_map/dynamic_slice | solution.py:541
  64.4 6.1 %collective-permute-done.10.refs_2_ = f32[1,24,384]{2,1,0:T(8,128)S(1)} collective-permute-done((f32[1,24,384]{2,1,0:T(8,128)S(1)}, f32[1,24,384]{2,1,0:T(8,128)S(1)}, u32[]{:S(2)}, u32[]{:S(2)}) %collective-permute-start.10) | collective-permute-done | bytes 36896 | tf_op jit(solution)/shard_map/ppermute | solution.py:468
  70.5 0.0 collective-permute-done.11.refs_3_
  70.5 0.0 collective-permute-done.9.refs_1_
  70.5 0.0 collective-permute-done.14.refs_6_
  70.5 0.0 collective-permute-done.15.refs_7_
  70.5 1.3 %update.1 = (f32[256,768]{1,0:T(8,128)}, f32[1,16,384]{2,1,0:T(8,128)}) custom-call(bf16[256,768]{1,0:T(8,128)(2,1)S(1)} %constant_dynamic-slice_fusion.c_ref, f32[1,256]{1,0:T(1,128)S(1)} %bitcast.7, f32[1,24,384]{2,1,0:T(8,128)S(1)} %get-tuple-element.59.refs_2_.refs_0_, f32[1,24,384]{2,1,0:T(8,128)S(1)} %collective-permute-done.9.refs_1_, ...), custom_call_target="tpu_custom_call" | custom-call | flops 1024 | bytes 1024 | tf_op jit(solution)/shard_map/update/pallas_call | solution.py:607
  (5 shorter events, 0.1 us)
Async XLA Ops:
  0.6 6.8 %collective-permute-start = (bf16[1024,768]{1,0:T(8,128)(2,1)}, bf16[1024,768]{1,0:T(8,128)(2,1)S(1)}, u32[]{:S(2)}, u32[]{:S(2)}) collective-permute-start(bf16[1024,768]{1,0:T(8,128)(2,1)} %v_ref.1), channel_id=1, source_target_pairs={{0,2},{2,0},{4,6},{6,4},{8,10},{10,8},{12,14},{14,12},{16,18},{18,... | collective-permute-start | bytes 4718600 | tf_op jit(solution)/shard_map/ppermute | solution.py:468
  7.4 4.4 %copy-start.2 = (s32[1024]{0:T(1024)S(1)}, s32[1024]{0:T(1024)}, u32[]{:S(2)}) copy-start(s32[1024]{0:T(1024)} %param.9) | copy-start | bytes 12292
  7.4 9.0 %copy-start = (bf16[768,768]{1,0:T(8,128)(2,1)S(1)}, bf16[768,768]{1,0:T(8,128)(2,1)}, u32[]{:S(2)}) copy-start(bf16[768,768]{1,0:T(8,128)(2,1)} %rot_ref.1) | copy-start | bytes 3538948
  7.5 9.0 %copy-start.1 = (s32[8192]{0:T(1024)S(1)}, s32[8192]{0:T(1024)}, u32[]{:S(2)}) copy-start(s32[8192]{0:T(1024)} %param.10) | copy-start | bytes 98308
  11.7 1.7 %collective-permute-start.1 = (f32[4,1024]{1,0:T(4,128)S(1)}, f32[4,1024]{1,0:T(4,128)S(1)}, u32[]{:S(2)}, u32[]{:S(2)}) collective-permute-start(f32[4,1024]{1,0:T(4,128)S(1)} %get-tuple-element.38._.a_ref), channel_id=1, source_target_pairs={{0,2},{2,0},{4,6},{6,4},{8,10},{10,8},{12,14},{14,12},{16,18},{18,... | collective-permute-start | bytes 49160 | tf_op jit(solution)/shard_map/ppermute | solution.py:468
  13.4 10.1 %collective-permute-start.2 = (f32[4,1024]{1,0:T(4,128)S(1)}, f32[4,1024]{1,0:T(4,128)S(1)}, u32[]{:S(2)}, u32[]{:S(2)}) collective-permute-start(f32[4,1024]{1,0:T(4,128)S(1)} %merge.1._.near_ref), channel_id=1, source_target_pairs={{0,1},{1,0},{2,3},{3,2},{4,5},{5,4},{6,7},{7,6},{8,9},{9,8},{10,11... | collective-permute-start | bytes 49160 | tf_op jit(solution)/shard_map/ppermute | solution.py:468
  25.2 8.7 %collective-permute-start.4 = (bf16[256,768]{1,0:T(8,128)(2,1)}, bf16[256,768]{1,0:T(8,128)(2,1)S(1)}, u32[]{:S(2)}, u32[]{:S(2)}) collective-permute-start(bf16[256,768]{1,0:T(8,128)(2,1)} %get-tuple-element.49), channel_id=1, source_target_pairs={{0,4},{2,10},{4,0},{6,14},{8,12},{10,2},{12,8},{14,6},{16,20},{18,... | collective-permute-start | bytes 1179656 | tf_op jit(solution)/shard_map/ppermute | solution.py:473
  30.3 6.5 %collective-permute-start.3 = (bf16[16,16,384]{2,1,0:T(8,128)(2,1)S(1)}, bf16[16,16,384]{2,1,0:T(8,128)(2,1)S(1)}, u32[]{:S(2)}, u32[]{:S(2)}) collective-permute-start(bf16[16,16,384]{2,1,0:T(8,128)(2,1)S(1)} %get-tuple-element.47), channel_id=1, source_target_pairs={{0,1},{1,0},{2,3},{3,2},{4,5},{5,4},{6,7},{7,6},{8,9},{9,8},{10,11... | collective-permute-start | bytes 589832 | tf_op jit(solution)/shard_map/ppermute | solution.py:468
  33.7 12.4 %collective-permute-start.7 = (bf16[256,768]{1,0:T(8,128)(2,1)}, bf16[256,768]{1,0:T(8,128)(2,1)S(1)}, u32[]{:S(2)}, u32[]{:S(2)}) collective-permute-start(bf16[256,768]{1,0:T(8,128)(2,1)} %get-tuple-element.58), channel_id=1, source_target_pairs={{0,4},{2,10},{4,0},{6,14},{8,12},{10,2},{12,8},{14,6},{16,20},{18,... | collective-permute-start | bytes 1179656 | tf_op jit(solution)/shard_map/ppermute | solution.py:473
  34.7 11.5 %collective-permute-start.8 = (bf16[256,768]{1,0:T(8,128)(2,1)}, bf16[256,768]{1,0:T(8,128)(2,1)S(1)}, u32[]{:S(2)}, u32[]{:S(2)}) collective-permute-start(bf16[256,768]{1,0:T(8,128)(2,1)} %added.3._), channel_id=1, source_target_pairs={{0,8},{2,6},{4,12},{6,2},{8,0},{10,14},{12,4},{14,10},{16,24},{18,... | collective-permute-start | bytes 1179656 | tf_op jit(solution)/shard_map/ppermute | solution.py:473
  41.1 11.6 %collective-permute-start.13 = (bf16[256,768]{1,0:T(8,128)(2,1)}, bf16[256,768]{1,0:T(8,128)(2,1)S(1)}, u32[]{:S(2)}, u32[]{:S(2)}) collective-permute-start(bf16[256,768]{1,0:T(8,128)(2,1)} %get-tuple-element.65), channel_id=1, source_target_pairs={{0,4},{2,10},{4,0},{6,14},{8,12},{10,2},{12,8},{14,6},{16,20},{18,... | collective-permute-start | bytes 1179656 | tf_op jit(solution)/shard_map/ppermute | solution.py:473
  42.6 1.4 %collective-permute-start.5 = (f32[8,16,384]{2,1,0:T(8,128)S(1)}, f32[8,16,384]{2,1,0:T(8,128)S(1)}, u32[]{:S(2)}, u32[]{:S(2)}) collective-permute-start(f32[8,16,384]{2,1,0:T(8,128)S(1)} %get-tuple-element.52), channel_id=1, source_target_pairs={{0,2},{2,0},{4,6},{6,4},{8,10},{10,8},{12,14},{14,12},{16,18},{18,... | collective-permute-start | bytes 589832 | tf_op jit(solution)/shard_map/ppermute | solution.py:468
  44.1 8.5 %collective-permute-start.6 = (f32[4,24,384]{2,1,0:T(8,128)S(1)}, f32[4,24,384]{2,1,0:T(8,128)S(1)}, u32[]{:S(2)}, u32[]{:S(2)}) collective-permute-start(f32[4,24,384]{2,1,0:T(8,128)S(1)} %get-tuple-element.56), channel_id=1, source_target_pairs={{0,4},{2,6},{4,0},{6,2},{8,12},{10,14},{12,8},{14,10},{16,20},{18,... | collective-permute-start | bytes 442376 | tf_op jit(solution)/shard_map/ppermute | solution.py:468
  44.7 15.0 %collective-permute-start.12 = (bf16[256,768]{1,0:T(8,128)(2,1)}, bf16[256,768]{1,0:T(8,128)(2,1)S(1)}, u32[]{:S(2)}, u32[]{:S(2)}) collective-permute-start(bf16[256,768]{1,0:T(8,128)(2,1)} %get-tuple-element.63), channel_id=1, source_target_pairs={{0,4},{2,10},{4,0},{6,14},{8,12},{10,2},{12,8},{14,6},{16,20},{18,... | collective-permute-start | bytes 1179656 | tf_op jit(solution)/shard_map/ppermute | solution.py:473
  47.1 23.4 %collective-permute-start.15 = (bf16[272,768]{1,0:T(8,128)(2,1)}, bf16[272,768]{1,0:T(8,128)(2,1)S(1)}, u32[]{:S(2)}, u32[]{:S(2)}) collective-permute-start(bf16[272,768]{1,0:T(8,128)(2,1)} %added.4.refs_2_), channel_id=1, source_target_pairs={{0,16},{2,18},{4,20},{6,22},{8,24},{10,26},{12,28},{14,30},{16,0},... | collective-permute-start | bytes 1253384 | tf_op jit(solution)/shard_map/ppermute | solution.py:473
  53.5 17.0 %collective-permute-start.14 = (bf16[256,768]{1,0:T(8,128)(2,1)}, bf16[256,768]{1,0:T(8,128)(2,1)S(1)}, u32[]{:S(2)}, u32[]{:S(2)}) collective-permute-start(bf16[256,768]{1,0:T(8,128)(2,1)} %added.5), channel_id=1, source_target_pairs={{0,8},{2,6},{4,12},{6,2},{8,0},{10,14},{12,4},{14,10},{16,24},{18,... | collective-permute-start | bytes 1179656 | tf_op jit(solution)/shard_map/ppermute | solution.py:473
  55.3 15.2 %collective-permute-start.10 = (f32[1,24,384]{2,1,0:T(8,128)S(1)}, f32[1,24,384]{2,1,0:T(8,128)S(1)}, u32[]{:S(2)}, u32[]{:S(2)}) collective-permute-start(f32[1,24,384]{2,1,0:T(8,128)S(1)} %get-tuple-element.61), channel_id=1, source_target_pairs={{0,16},{2,18},{4,20},{6,22},{8,24},{10,26},{12,28},{14,30},{16,0},... | collective-permute-start | bytes 110600 | tf_op jit(solution)/shard_map/ppermute | solution.py:468
  57.9 12.6 %collective-permute-start.11 = (f32[1,24,384]{2,1,0:T(8,128)S(1)}, f32[1,24,384]{2,1,0:T(8,128)S(1)}, u32[]{:S(2)}, u32[]{:S(2)}) collective-permute-start(f32[1,24,384]{2,1,0:T(8,128)S(1)} %get-tuple-element.62), channel_id=1, source_target_pairs={{0,24},{2,26},{4,28},{6,30},{8,16},{10,18},{12,20},{14,22},{16,8},... | collective-permute-start | bytes 110600 | tf_op jit(solution)/shard_map/ppermute | solution.py:468
  59.6 10.8 %collective-permute-start.9 = (f32[1,24,384]{2,1,0:T(8,128)S(1)}, f32[1,24,384]{2,1,0:T(8,128)S(1)}, u32[]{:S(2)}, u32[]{:S(2)}) collective-permute-start(f32[1,24,384]{2,1,0:T(8,128)S(1)} %get-tuple-element.60), channel_id=1, source_target_pairs={{0,8},{2,10},{4,12},{6,14},{8,0},{10,2},{12,4},{14,6},{16,24},{18,... | collective-permute-start | bytes 110600 | tf_op jit(solution)/shard_map/ppermute | solution.py:468

commit v4 on v3

--- a/solution.py
+++ b/solution.py
@@ -251,7 +251,7 @@
         + [pltpu.VMEM((size, width), F32) for size in rows[sends:]]
         + [jax.ShapeDtypeStruct(old.shape, F32)],
         scratch_shapes=[pltpu.VMEM((size, width), BF16) for size in rows[:sends]]
-        + [pltpu.SemaphoreType.DMA((sends,))],
+        + [pltpu.SemaphoreType.DMA((max(sends, 1),))],
         compiler_params=params(14),
         cost_estimate=cost(0),
         name="sums",
@@ -582,8 +582,9 @@
         theirs = jnp.zeros_like(mine)
     keep, sent = by_core(mine, theirs, in_hbm(next3))
     moments = [keep, flip(sent, "dp", 1)]
-    got1, got0, kept1, kept0, mass = sums(mass, ("send1", "send0", "keep1", "keep0"), keep)
+    got1, got0, mass = sums(mass, ("send1", "send0"), keep)
     came1, came0 = exchange(got1, 0), exchange(got0, 0)
+    kept1, kept0, mass = sums(mass, ("keep1", "keep0"), keep)
 
     keep, sent = packed(moments, mass, kept0)
     small = [keep, flip(sent, "dp", 2)]

time: 72 us -> 71.9 us (level)
  waiting for transfers between devices: 12.1 us -> 11.2 us
    ppermute x9, waiting for transfers between devices: 10.4 us -> 7.3 us  [flip(): return lax.ppermute(array, axis, [(i, i ^ mask) for i in range(size)])]
    ppermute x7, waiting for transfers between devices: 1.7 us -> 3.86 us  [exchange(): return lax.ppermute(array, 'dp', [(i, i ^ far[i % 2]) for i in range(size)])]
    ppermute x7, starting transfers between devices: 11.3 us -> 12.2 us  [exchange(): return lax.ppermute(array, 'dp', [(i, i ^ far[i % 2]) for i in range(size)])]
    pallas_call x3 -> x4, Pallas kernels: 8.73 us -> 9.14 us  [sums_of(): pl.pallas_call(functools.partial(sums_kernel, which=which, sends=sends, r...]
  transfers between devices with their start and end apart: 16 -> 16, of which waited for: 4 -> 5; matrix products, arithmetic and copies ran while one was open for 2% -> 2% of each run, Pallas kernels for 39% -> 40%
where the time goes in v4:
time: 71.9 us; the launch traced here: 71.6 us
  Pallas kernels  35.7 us (50%)
  starting transfers between devices  22.1 us (31%)
  waiting for transfers between devices  11.2 us (16%)
  local copies, waits for them, and re-layouts  1.81 us (3%)
  between operations  0.83 us (1%)
    ppermute x7, starting transfers between devices, exchange(): return lax.ppermute(array, 'dp', [(i, i ^ far[i % 2]) for i in range(size)])  12.2 us
    ppermute x9, starting transfers between devices, flip(): return lax.ppermute(array, axis, [(i, i ^ mask) for i in range(size)])  9.86 us
    pallas_call x4, Pallas kernels, sums_of(): pl.pallas_call(functools.partial(sums_kernel, which=which, sends=sends, r...  9.14 us
    ppermute x9, waiting for transfers between devices, flip(): return lax.ppermute(array, axis, [(i, i ^ mask) for i in range(size)])  7.3 us
    pallas_call x1, Pallas kernels, rotated_residuals(): pl.pallas_call(functools.partial(residual_kernel, places=places), in_spec...  7.01 us
    pallas_call x1, Pallas kernels, first_scores(): pl.pallas_call(functools.partial(first_scores_kernel, places=places, scal...  6.27 us
    pallas_call x1, Pallas kernels, second_scores(): pl.pallas_call(functools.partial(second_scores_kernel, scale=scale), in_s...  4.21 us
    ppermute x7, waiting for transfers between devices, exchange(): return lax.ppermute(array, 'dp', [(i, i ^ far[i % 2]) for i in range(size)])  3.86 us
  transfers between devices with their start and end apart: 16, of which 5 were waited for; matrix products, arithmetic and copies ran while one was open for 2% of the time, Pallas kernels for 40%

profile of v4, /device:TPU:0, one launch (start us, length us, event | category | flops | bytes accessed | tf_op | source)
XLA Modules:
  0.0 71.6 jit_solution(13104291644327231530)
XLA Ops:
  0.6 0.5 collective-permute-start
  1.1 6.3 %first_scores.1 = (f32[2048,1024]{1,0:T(8,128)S(1)}, f32[2,1024]{1,0:T(2,128)S(1)}, bf16[2048,768]{1,0:T(8,128)(2,1)S(1)}, bf16[1024,768]{1,0:T(8,128)(2,1)S(1)}) custom-call(bf16[1024,768]{1,0:T(8,128)(2,1)} %v_ref.1, bf16[16,256,768]{2,1,0:T(8,128)(2,1)} %bitcast.8), custom_call_target="tpu_custom_call" | custom-call | flops 1024 | bytes 1024 | tf_op jit(solution)/shard_map/first_scores/pallas_call | solution.py:129
  7.4 0.0 copy-start.2
  7.4 0.0 collective-permute-done.v_ref.v2_ref
  7.4 0.0 copy-start
  7.5 0.0 copy-start.1
  7.5 4.2 %second_scores.1 = (f32[2048,1024]{1,0:T(8,128)S(1)}, f32[4,1024]{1,0:T(4,128)S(1)}) custom-call(bf16[1024,768]{1,0:T(8,128)(2,1)S(1)} %collective-permute-done.v_ref.v2_ref, bf16[2048,768]{1,0:T(8,128)(2,1)S(1)} %get-tuple-element.37.ch_ref.near_ref, f32[2,1024]{1,0:T(2,128)S(1)} %get-tuple-element.38.st_ref), custom_call_target="tpu_custom_call" | custom-call | flops 1024 | bytes 1024 | tf_op jit(solution)/shard_map/second_scores/pallas_call | solution.py:156
  11.7 0.1 collective-permute-start.1
  11.8 0.0 copy-done.2
  11.8 1.6 %picked.1 = (bf16[512,768]{1,0:T(8,128)(2,1)S(1)}, s32[512,128]{1,0:T(8,128)S(1)}) custom-call(s32[1,1024]{1,0:T(1,128)S(1)} %bitcast.6, bf16[1024,768]{1,0:T(8,128)(2,1)S(1)} %get-tuple-element.36.v_ref.v1_ref, f32[4,1024]{1,0:T(4,128)S(1)} %get-tuple-element.39._.a_ref), custom_call_target="tpu_custom_call" | custom-call | flops 1024 | bytes 1024 | tf_op jit(solution)/shard_map/picked/pallas_call | solution.py:280
  13.3 0.0 collective-permute-done.1.b_ref
  13.4 3.0 %collective-permute-start.2 = (f32[4,1024]{1,0:T(4,128)S(1)}, f32[4,1024]{1,0:T(4,128)S(1)}, u32[]{:S(2)}, u32[]{:S(2)}) collective-permute-start(f32[4,1024]{1,0:T(4,128)S(1)} %merge.1._.near_ref), channel_id=1, source_target_pairs={{0,1},{1,0},{2,3},{3,2},{4,5},{5,4},{6,7},{7,6},{8,9},{9,8},{10,11... | collective-permute-start | bytes 49160 | tf_op jit(solution)/shard_map/ppermute | solution.py:468
  16.4 0.0 copy-done
  16.4 0.0 copy-done.1
  16.4 7.0 %residuals.1 = (bf16[512,768]{1,0:T(8,128)(2,1)S(1)}, f32[512,128]{1,0:T(8,128)S(1)}) custom-call(bf16[512,768]{1,0:T(8,128)(2,1)S(1)} %get-tuple-element.40.picked_ref, s32[512,128]{1,0:T(8,128)S(1)} %get-tuple-element.41._.ids_ref, bf16[2048,768]{1,0:T(8,128)(2,1)S(1)} %get-tuple-element.37.ch_ref.near_ref, bf16[16,256,768]{2,1,0:T(8,128)(2,1)} %bitcast.9, ...), custom_call_target="tpu_custom_call" | custom-call | flops 1024 | bytes 1024 | tf_op jit(solution)/shard_map/residuals/pallas_call | solution.py:337
  23.4 0.0 collective-permute-done.2.far_ref
  23.5 1.7 %sums.4 = (bf16[256,768]{1,0:T(8,128)(2,1)}, f32[8,256]{1,0:T(8,128)S(1)}) custom-call(f32[2048,1024]{1,0:T(8,128)S(1)} %get-tuple-element.44.s1_ref.__, f32[2048,1024]{1,0:T(8,128)S(1)} %get-tuple-element.45.s2_ref.___, f32[4,1024]{1,0:T(4,128)S(1)} %merge.1._.near_ref, f32[4,1024]{1,0:T(4,128)S(1)} %collective-permute-done.2.far_ref, ...), custom_call_target="tpu_custom_call" | custom-call | flops 1024 | bytes 1024 | tf_op jit(solution)/shard_map/sums/pallas_call | solution.py:246
  25.2 1.6 %collective-permute-start.4 = (bf16[256,768]{1,0:T(8,128)(2,1)}, bf16[256,768]{1,0:T(8,128)(2,1)S(1)}, u32[]{:S(2)}, u32[]{:S(2)}) collective-permute-start(bf16[256,768]{1,0:T(8,128)(2,1)} %get-tuple-element.50), channel_id=1, source_target_pairs={{0,4},{2,10},{4,0},{6,14},{8,12},{10,2},{12,8},{14,6},{16,20},{18,... | collective-permute-start | bytes 1179656 | tf_op jit(solution)/shard_map/ppermute | solution.py:473
  26.8 3.6 %moments.1 = (f32[16,16,384]{2,1,0:T(8,128)S(1)}, bf16[16,16,384]{2,1,0:T(8,128)(2,1)S(1)}) custom-call(bf16[512,768]{1,0:T(8,128)(2,1)S(1)} %get-tuple-element.42.r_ref, f32[512,128]{1,0:T(8,128)S(1)} %get-tuple-element.43._.own_ref, f32[8,256]{1,0:T(8,128)S(1)} %get-tuple-element.46._.old_ref, f32[2048,1024]{1,0:T(8,128)S(1)} %get-tuple-element.44.s1_ref.__, ...), custom_call_target="tpu_custom_call" | custom-call | flops 1024 | bytes 1024 | tf_op jit(solution)/shard_map/moments/pallas_call | solution.py:383
  30.3 0.6 collective-permute-start.3
  30.9 2.8 %sums.5 = (bf16[256,768]{1,0:T(8,128)(2,1)}, f32[256,768]{1,0:T(8,128)S(1)}, f32[256,768]{1,0:T(8,128)S(1)}, f32[8,256]{1,0:T(8,128)S(1)}) custom-call(f32[2048,1024]{1,0:T(8,128)S(1)} %get-tuple-element.44.s1_ref.__, f32[2048,1024]{1,0:T(8,128)S(1)} %get-tuple-element.45.s2_ref.___, f32[4,1024]{1,0:T(4,128)S(1)} %merge.1._.near_ref, ...), custom_call_target="tpu_custom_call" | custom-call | flops 1024 | bytes 1024 | tf_op jit(solution)/shard_map/sums/pallas_call | solution.py:246
  33.7 0.1 collective-permute-start.7
  33.9 0.0 collective-permute-done.4.refs_1_
  33.9 0.8 %added.3._ = bf16[256,768]{1,0:T(8,128)(2,1)} custom-call(f32[256,768]{1,0:T(8,128)S(1)} %get-tuple-element.49.refs_0_, bf16[256,768]{1,0:T(8,128)(2,1)S(1)} %collective-permute-done.4.refs_1_, f32[8,256]{1,0:T(8,128)S(1)} %get-tuple-element.51.refs_2_.old_ref), custom_call_target="tpu_custom_call" | custom-call | flops 1024 | bytes 1024 | tf_op jit(solution)/shard_map/added/pallas_call | solution.py:496
  34.7 2.1 %collective-permute-start.8 = (bf16[256,768]{1,0:T(8,128)(2,1)}, bf16[256,768]{1,0:T(8,128)(2,1)S(1)}, u32[]{:S(2)}, u32[]{:S(2)}) collective-permute-start(bf16[256,768]{1,0:T(8,128)(2,1)} %added.3._), channel_id=1, source_target_pairs={{0,8},{2,6},{4,12},{6,2},{8,0},{10,14},{12,4},{14,10},{16,24},{18,... | collective-permute-start | bytes 1179656 | tf_op jit(solution)/shard_map/ppermute | solution.py:473
  36.8 0.0 collective-permute-done.3.b_ref
  36.9 2.7 %sums.6 = (bf16[256,768]{1,0:T(8,128)(2,1)}, bf16[256,768]{1,0:T(8,128)(2,1)}, f32[8,256]{1,0:T(8,128)S(1)}) custom-call(f32[2048,1024]{1,0:T(8,128)S(1)} %get-tuple-element.44.s1_ref.__, f32[2048,1024]{1,0:T(8,128)S(1)} %get-tuple-element.45.s2_ref.___, f32[4,1024]{1,0:T(4,128)S(1)} %merge.1._.near_ref, f32[4,1024]{1,0:T(4,128)S(1)} %collective-permute-done.2.far_ref, ...), custom_call_target="tpu_custom_call" | custom-call | flops 1024 | bytes 1024 | tf_op jit(solution)/shard_map/sums/pallas_call | solution.py:246
  39.6 1.6 %collective-permute-start.13 = (bf16[256,768]{1,0:T(8,128)(2,1)}, bf16[256,768]{1,0:T(8,128)(2,1)S(1)}, u32[]{:S(2)}, u32[]{:S(2)}) collective-permute-start(bf16[256,768]{1,0:T(8,128)(2,1)} %get-tuple-element.67), channel_id=1, source_target_pairs={{0,4},{2,10},{4,0},{6,14},{8,12},{10,2},{12,8},{14,6},{16,20},{18,... | collective-permute-start | bytes 1179656 | tf_op jit(solution)/shard_map/ppermute | solution.py:473
  41.1 0.0 collective-permute-start.5
  41.1 0.0 copy-start.3
  41.1 1.9 %sums.7 = (f32[256,768]{1,0:T(8,128)S(1)}, f32[256,768]{1,0:T(8,128)S(1)}, f32[8,256]{1,0:T(8,128)S(1)}) custom-call(f32[2048,1024]{1,0:T(8,128)S(1)} %get-tuple-element.44.s1_ref.__, f32[2048,1024]{1,0:T(8,128)S(1)} %get-tuple-element.45.s2_ref.___, f32[4,1024]{1,0:T(4,128)S(1)} %merge.1._.near_ref, f32[4,1024]{1,0:T(4,128)S(1)} %collective-permute-done.2.far_ref, ...), custom_call_target="tpu_custom_call" | custom-call | flops 1024 | bytes 1024 | tf_op jit(solution)/shard_map/sums/pallas_call | solution.py:246
  43.1 0.0 collective-permute-done.5.refs_1_
  43.1 0.6 collective-permute-start.6
  43.7 0.0 copy-done.3
  43.7 1.5 %collective-permute-start.12 = (bf16[256,768]{1,0:T(8,128)(2,1)S(1)}, bf16[256,768]{1,0:T(8,128)(2,1)S(1)}, u32[]{:S(2)}, u32[]{:S(2)}) collective-permute-start(bf16[256,768]{1,0:T(8,128)(2,1)S(1)} %copy-done.3), channel_id=1, source_target_pairs={{0,4},{2,10},{4,0},{6,14},{8,12},{10,2},{12,8},{14,6},{16,20},{18,... | collective-permute-start | bytes 1179656 | tf_op jit(solution)/shard_map/ppermute | solution.py:473
  45.2 0.1 collective-permute-done.7.refs_1_
  45.3 1.8 %collective-permute-done.8.refs_2_ = bf16[256,768]{1,0:T(8,128)(2,1)S(1)} collective-permute-done((bf16[256,768]{1,0:T(8,128)(2,1)}, bf16[256,768]{1,0:T(8,128)(2,1)S(1)}, u32[]{:S(2)}, u32[]{:S(2)}) %collective-permute-start.8) | collective-permute-done | bytes 393248 | tf_op jit(solution)/shard_map/ppermute | solution.py:473
  47.1 0.9 %added.4.refs_2_ = bf16[272,768]{1,0:T(8,128)(2,1)} custom-call(f32[256,768]{1,0:T(8,128)S(1)} %get-tuple-element.59.refs_0_, bf16[256,768]{1,0:T(8,128)(2,1)S(1)} %collective-permute-done.7.refs_1_, bf16[256,768]{1,0:T(8,128)(2,1)S(1)} %collective-permute-done.8.refs_2_, f32[4,24,384]{2,1,0:T(8,128)S(1)} %get-tuple-element.57.refs_3_.refs_0_), custom_call_target="tpu_custom_call" | custom-call | flops 1024 | bytes 1024 | tf_op jit(solution)/shard_map/added/pallas_call | solution.py:496
  48.0 3.1 %collective-permute-start.15 = (bf16[272,768]{1,0:T(8,128)(2,1)}, bf16[272,768]{1,0:T(8,128)(2,1)S(1)}, u32[]{:S(2)}, u32[]{:S(2)}) collective-permute-start(bf16[272,768]{1,0:T(8,128)(2,1)} %added.4.refs_2_), channel_id=1, source_target_pairs={{0,16},{2,18},{4,20},{6,22},{8,24},{10,26},{12,28},{14,30},{16,0},... | collective-permute-start | bytes 1253384 | tf_op jit(solution)/shard_map/ppermute | solution.py:473
  51.1 1.6 %collective-permute-done.6.refs_1_ = f32[4,24,384]{2,1,0:T(8,128)S(1)} collective-permute-done((f32[4,24,384]{2,1,0:T(8,128)S(1)}, f32[4,24,384]{2,1,0:T(8,128)S(1)}, u32[]{:S(2)}, u32[]{:S(2)}) %collective-permute-start.6) | collective-permute-done | bytes 147488 | tf_op jit(solution)/shard_map/ppermute | solution.py:468
  52.7 0.0 collective-permute-done.13.refs_1_
  52.7 0.8 %added.5 = bf16[256,768]{1,0:T(8,128)(2,1)} custom-call(f32[256,768]{1,0:T(8,128)S(1)} %get-tuple-element.66.refs_0_, bf16[256,768]{1,0:T(8,128)(2,1)S(1)} %collective-permute-done.13.refs_1_, f32[1,24,384]{2,1,0:T(8,128)S(1)} %get-tuple-element.61.refs_2_.refs_0_), custom_call_target="tpu_custom_call" | custom-call | flops 1024 | bytes 1024 | tf_op jit(solution)/shard_map/added/pallas_call | solution.py:496
  53.5 2.3 %collective-permute-start.14 = (bf16[256,768]{1,0:T(8,128)(2,1)}, bf16[256,768]{1,0:T(8,128)(2,1)S(1)}, u32[]{:S(2)}, u32[]{:S(2)}) collective-permute-start(bf16[256,768]{1,0:T(8,128)(2,1)} %added.5), channel_id=1, source_target_pairs={{0,8},{2,6},{4,12},{6,2},{8,0},{10,14},{12,4},{14,10},{16,24},{18,... | collective-permute-start | bytes 1179656 | tf_op jit(solution)/shard_map/ppermute | solution.py:473
  55.8 2.5 %collective-permute-start.10 = (f32[1,24,384]{2,1,0:T(8,128)S(1)}, f32[1,24,384]{2,1,0:T(8,128)S(1)}, u32[]{:S(2)}, u32[]{:S(2)}) collective-permute-start(f32[1,24,384]{2,1,0:T(8,128)S(1)} %get-tuple-element.63), channel_id=1, source_target_pairs={{0,16},{2,18},{4,20},{6,22},{8,24},{10,26},{12,28},{14,30},{16,0},... | collective-permute-start | bytes 110600 | tf_op jit(solution)/shard_map/ppermute | solution.py:468
  58.3 0.0 collective-permute-start.11
  58.3 2.0 %collective-permute-done.12.refs_5_ = bf16[256,768]{1,0:T(8,128)(2,1)S(1)} collective-permute-done((bf16[256,768]{1,0:T(8,128)(2,1)S(1)}, bf16[256,768]{1,0:T(8,128)(2,1)S(1)}, u32[]{:S(2)}, u32[]{:S(2)}) %collective-permute-start.12) | collective-permute-done | bytes 393248 | tf_op jit(solution)/shard_map/ppermute | solution.py:473
  60.3 2.5 %collective-permute-start.9 = (f32[1,24,384]{2,1,0:T(8,128)S(1)}, f32[1,24,384]{2,1,0:T(8,128)S(1)}, u32[]{:S(2)}, u32[]{:S(2)}) collective-permute-start(f32[1,24,384]{2,1,0:T(8,128)S(1)} %get-tuple-element.62), channel_id=1, source_target_pairs={{0,8},{2,10},{4,12},{6,14},{8,0},{10,2},{12,4},{14,6},{16,24},{18,... | collective-permute-start | bytes 110600 | tf_op jit(solution)/shard_map/ppermute | solution.py:468
  62.8 1.0 %constant_dynamic-slice_fusion.c_ref = bf16[256,768]{1,0:T(8,128)(2,1)S(1)} fusion(bf16[4096,768]{1,0:T(8,128)(2,1)} %param.7, s32[]{:T(128)S(6)} %select_n.4), kind=kLoop, calls=%fused_computation | loop fusion | bytes 786436 | tf_op jit(solution)/shard_map/dynamic_slice | solution.py:540
  63.8 0.8 %dynamic_slice.7 = f32[256]{0:T(256)S(1)} dynamic-slice(f32[4096]{0:T(1024)} %param.8, s32[]{:T(128)S(6)} %select_n.4), dynamic_slice_sizes={256} | dynamic-slice | bytes 2052 | tf_op jit(solution)/shard_map/dynamic_slice | solution.py:541
  64.6 5.7 %collective-permute-done.10.refs_2_ = f32[1,24,384]{2,1,0:T(8,128)S(1)} collective-permute-done((f32[1,24,384]{2,1,0:T(8,128)S(1)}, f32[1,24,384]{2,1,0:T(8,128)S(1)}, u32[]{:S(2)}, u32[]{:S(2)}) %collective-permute-start.10) | collective-permute-done | bytes 36896 | tf_op jit(solution)/shard_map/ppermute | solution.py:468
  70.3 0.0 collective-permute-done.11.refs_3_
  70.3 0.0 collective-permute-done.9.refs_1_
  70.3 0.0 collective-permute-done.14.refs_6_
  70.3 0.0 collective-permute-done.15.refs_7_
  70.3 1.3 %update.1 = (f32[256,768]{1,0:T(8,128)}, f32[1,16,384]{2,1,0:T(8,128)}) custom-call(bf16[256,768]{1,0:T(8,128)(2,1)S(1)} %constant_dynamic-slice_fusion.c_ref, f32[1,256]{1,0:T(1,128)S(1)} %bitcast.7, f32[1,24,384]{2,1,0:T(8,128)S(1)} %get-tuple-element.61.refs_2_.refs_0_, f32[1,24,384]{2,1,0:T(8,128)S(1)} %collective-permute-done.9.refs_1_, ...), custom_call_target="tpu_custom_call" | custom-call | flops 1024 | bytes 1024 | tf_op jit(solution)/shard_map/update/pallas_call | solution.py:608
  (5 shorter events, 0.1 us)
Async XLA Ops:
  0.6 6.8 %collective-permute-start = (bf16[1024,768]{1,0:T(8,128)(2,1)}, bf16[1024,768]{1,0:T(8,128)(2,1)S(1)}, u32[]{:S(2)}, u32[]{:S(2)}) collective-permute-start(bf16[1024,768]{1,0:T(8,128)(2,1)} %v_ref.1), channel_id=1, source_target_pairs={{0,2},{2,0},{4,6},{6,4},{8,10},{10,8},{12,14},{14,12},{16,18},{18,... | collective-permute-start | bytes 4718600 | tf_op jit(solution)/shard_map/ppermute | solution.py:468
  7.4 4.4 %copy-start.2 = (s32[1024]{0:T(1024)S(1)}, s32[1024]{0:T(1024)}, u32[]{:S(2)}) copy-start(s32[1024]{0:T(1024)} %param.9) | copy-start | bytes 12292
  7.4 9.0 %copy-start = (bf16[768,768]{1,0:T(8,128)(2,1)S(1)}, bf16[768,768]{1,0:T(8,128)(2,1)}, u32[]{:S(2)}) copy-start(bf16[768,768]{1,0:T(8,128)(2,1)} %rot_ref.1) | copy-start | bytes 3538948
  7.5 9.0 %copy-start.1 = (s32[8192]{0:T(1024)S(1)}, s32[8192]{0:T(1024)}, u32[]{:S(2)}) copy-start(s32[8192]{0:T(1024)} %param.10) | copy-start | bytes 98308
  11.7 1.7 %collective-permute-start.1 = (f32[4,1024]{1,0:T(4,128)S(1)}, f32[4,1024]{1,0:T(4,128)S(1)}, u32[]{:S(2)}, u32[]{:S(2)}) collective-permute-start(f32[4,1024]{1,0:T(4,128)S(1)} %get-tuple-element.39._.a_ref), channel_id=1, source_target_pairs={{0,2},{2,0},{4,6},{6,4},{8,10},{10,8},{12,14},{14,12},{16,18},{18,... | collective-permute-start | bytes 49160 | tf_op jit(solution)/shard_map/ppermute | solution.py:468
  13.4 10.1 %collective-permute-start.2 = (f32[4,1024]{1,0:T(4,128)S(1)}, f32[4,1024]{1,0:T(4,128)S(1)}, u32[]{:S(2)}, u32[]{:S(2)}) collective-permute-start(f32[4,1024]{1,0:T(4,128)S(1)} %merge.1._.near_ref), channel_id=1, source_target_pairs={{0,1},{1,0},{2,3},{3,2},{4,5},{5,4},{6,7},{7,6},{8,9},{9,8},{10,11... | collective-permute-start | bytes 49160 | tf_op jit(solution)/shard_map/ppermute | solution.py:468
  25.2 8.7 %collective-permute-start.4 = (bf16[256,768]{1,0:T(8,128)(2,1)}, bf16[256,768]{1,0:T(8,128)(2,1)S(1)}, u32[]{:S(2)}, u32[]{:S(2)}) collective-permute-start(bf16[256,768]{1,0:T(8,128)(2,1)} %get-tuple-element.50), channel_id=1, source_target_pairs={{0,4},{2,10},{4,0},{6,14},{8,12},{10,2},{12,8},{14,6},{16,20},{18,... | collective-permute-start | bytes 1179656 | tf_op jit(solution)/shard_map/ppermute | solution.py:473
  30.3 6.5 %collective-permute-start.3 = (bf16[16,16,384]{2,1,0:T(8,128)(2,1)S(1)}, bf16[16,16,384]{2,1,0:T(8,128)(2,1)S(1)}, u32[]{:S(2)}, u32[]{:S(2)}) collective-permute-start(bf16[16,16,384]{2,1,0:T(8,128)(2,1)S(1)} %get-tuple-element.48), channel_id=1, source_target_pairs={{0,1},{1,0},{2,3},{3,2},{4,5},{5,4},{6,7},{7,6},{8,9},{9,8},{10,11... | collective-permute-start | bytes 589832 | tf_op jit(solution)/shard_map/ppermute | solution.py:468
  33.7 11.5 %collective-permute-start.7 = (bf16[256,768]{1,0:T(8,128)(2,1)}, bf16[256,768]{1,0:T(8,128)(2,1)S(1)}, u32[]{:S(2)}, u32[]{:S(2)}) collective-permute-start(bf16[256,768]{1,0:T(8,128)(2,1)} %get-tuple-element.60), channel_id=1, source_target_pairs={{0,4},{2,10},{4,0},{6,14},{8,12},{10,2},{12,8},{14,6},{16,20},{18,... | collective-permute-start | bytes 1179656 | tf_op jit(solution)/shard_map/ppermute | solution.py:473
  34.7 12.4 %collective-permute-start.8 = (bf16[256,768]{1,0:T(8,128)(2,1)}, bf16[256,768]{1,0:T(8,128)(2,1)S(1)}, u32[]{:S(2)}, u32[]{:S(2)}) collective-permute-start(bf16[256,768]{1,0:T(8,128)(2,1)} %added.3._), channel_id=1, source_target_pairs={{0,8},{2,6},{4,12},{6,2},{8,0},{10,14},{12,4},{14,10},{16,24},{18,... | collective-permute-start | bytes 1179656 | tf_op jit(solution)/shard_map/ppermute | solution.py:473
  39.6 13.1 %collective-permute-start.13 = (bf16[256,768]{1,0:T(8,128)(2,1)}, bf16[256,768]{1,0:T(8,128)(2,1)S(1)}, u32[]{:S(2)}, u32[]{:S(2)}) collective-permute-start(bf16[256,768]{1,0:T(8,128)(2,1)} %get-tuple-element.67), channel_id=1, source_target_pairs={{0,4},{2,10},{4,0},{6,14},{8,12},{10,2},{12,8},{14,6},{16,20},{18,... | collective-permute-start | bytes 1179656 | tf_op jit(solution)/shard_map/ppermute | solution.py:473
  41.1 1.9 %collective-permute-start.5 = (f32[8,16,384]{2,1,0:T(8,128)S(1)}, f32[8,16,384]{2,1,0:T(8,128)S(1)}, u32[]{:S(2)}, u32[]{:S(2)}) collective-permute-start(f32[8,16,384]{2,1,0:T(8,128)S(1)} %get-tuple-element.53), channel_id=1, source_target_pairs={{0,2},{2,0},{4,6},{6,4},{8,10},{10,8},{12,14},{14,12},{16,18},{18,... | collective-permute-start | bytes 589832 | tf_op jit(solution)/shard_map/ppermute | solution.py:468
  41.1 2.6 %copy-start.3 = (bf16[256,768]{1,0:T(8,128)(2,1)S(1)}, bf16[256,768]{1,0:T(8,128)(2,1)}, u32[]{:S(2)}) copy-start(bf16[256,768]{1,0:T(8,128)(2,1)} %get-tuple-element.65) | copy-start | bytes 1179652
  43.1 9.5 %collective-permute-start.6 = (f32[4,24,384]{2,1,0:T(8,128)S(1)}, f32[4,24,384]{2,1,0:T(8,128)S(1)}, u32[]{:S(2)}, u32[]{:S(2)}) collective-permute-start(f32[4,24,384]{2,1,0:T(8,128)S(1)} %get-tuple-element.58), channel_id=1, source_target_pairs={{0,4},{2,6},{4,0},{6,2},{8,12},{10,14},{12,8},{14,10},{16,20},{18,... | collective-permute-start | bytes 442376 | tf_op jit(solution)/shard_map/ppermute | solution.py:468
  43.7 16.6 %collective-permute-start.12 = (bf16[256,768]{1,0:T(8,128)(2,1)S(1)}, bf16[256,768]{1,0:T(8,128)(2,1)S(1)}, u32[]{:S(2)}, u32[]{:S(2)}) collective-permute-start(bf16[256,768]{1,0:T(8,128)(2,1)S(1)} %copy-done.3), channel_id=1, source_target_pairs={{0,4},{2,10},{4,0},{6,14},{8,12},{10,2},{12,8},{14,6},{16,20},{18,... | collective-permute-start | bytes 1179656 | tf_op jit(solution)/shard_map/ppermute | solution.py:473
  48.0 22.3 %collective-permute-start.15 = (bf16[272,768]{1,0:T(8,128)(2,1)}, bf16[272,768]{1,0:T(8,128)(2,1)S(1)}, u32[]{:S(2)}, u32[]{:S(2)}) collective-permute-start(bf16[272,768]{1,0:T(8,128)(2,1)} %added.4.refs_2_), channel_id=1, source_target_pairs={{0,16},{2,18},{4,20},{6,22},{8,24},{10,26},{12,28},{14,30},{16,0},... | collective-permute-start | bytes 1253384 | tf_op jit(solution)/shard_map/ppermute | solution.py:473
  53.5 16.8 %collective-permute-start.14 = (bf16[256,768]{1,0:T(8,128)(2,1)}, bf16[256,768]{1,0:T(8,128)(2,1)S(1)}, u32[]{:S(2)}, u32[]{:S(2)}) collective-permute-start(bf16[256,768]{1,0:T(8,128)(2,1)} %added.5), channel_id=1, source_target_pairs={{0,8},{2,6},{4,12},{6,2},{8,0},{10,14},{12,4},{14,10},{16,24},{18,... | collective-permute-start | bytes 1179656 | tf_op jit(solution)/shard_map/ppermute | solution.py:473
  55.8 14.5 %collective-permute-start.10 = (f32[1,24,384]{2,1,0:T(8,128)S(1)}, f32[1,24,384]{2,1,0:T(8,128)S(1)}, u32[]{:S(2)}, u32[]{:S(2)}) collective-permute-start(f32[1,24,384]{2,1,0:T(8,128)S(1)} %get-tuple-element.63), channel_id=1, source_target_pairs={{0,16},{2,18},{4,20},{6,22},{8,24},{10,26},{12,28},{14,30},{16,0},... | collective-permute-start | bytes 110600 | tf_op jit(solution)/shard_map/ppermute | solution.py:468
  58.3 11.9 %collective-permute-start.11 = (f32[1,24,384]{2,1,0:T(8,128)S(1)}, f32[1,24,384]{2,1,0:T(8,128)S(1)}, u32[]{:S(2)}, u32[]{:S(2)}) collective-permute-start(f32[1,24,384]{2,1,0:T(8,128)S(1)} %get-tuple-element.64), channel_id=1, source_target_pairs={{0,24},{2,26},{4,28},{6,30},{8,16},{10,18},{12,20},{14,22},{16,8},... | collective-permute-start | bytes 110600 | tf_op jit(solution)/shard_map/ppermute | solution.py:468
  60.3 10.0 %collective-permute-start.9 = (f32[1,24,384]{2,1,0:T(8,128)S(1)}, f32[1,24,384]{2,1,0:T(8,128)S(1)}, u32[]{:S(2)}, u32[]{:S(2)}) collective-permute-start(f32[1,24,384]{2,1,0:T(8,128)S(1)} %get-tuple-element.62), channel_id=1, source_target_pairs={{0,8},{2,10},{4,12},{6,14},{8,0},{10,2},{12,4},{14,6},{16,24},{18,... | collective-permute-start | bytes 110600 | tf_op jit(solution)/shard_map/ppermute | solution.py:468
